TPU v7x, 512 devices: a whole 4x4x16 slice. The times are simulated.
512 devices in a mesh: ctx: 32 (over z_lo, x), kvh: 4 (over y), dp: 4 (over z_hi, core).
Axes of the slice: x: 4, y: 4, z: 16 (z_hi: 2, z_lo: 8; z = z_hi * 8 + z_lo), core: 2. Of those that a mesh axis runs over, the one named last changes fastest.
Arguments:
- queries: bfloat16 [4, 4096, 32, 128], P('dp', 'ctx', 'kvh'), may hold values from -4 to 4
- keys: bfloat16 [4, 4096, 4, 128], P('dp', 'ctx', 'kvh'), may hold values from -4 to 4
- values: bfloat16 [4, 4096, 4, 128], P('dp', 'ctx', 'kvh'), may hold values from -6 to 6
- d_out: bfloat16 [4, 4096, 32, 128], P('dp', 'ctx', 'kvh'), may hold values from -6 to 6
- head_scale: float32 [32], replicated, may hold values from 1 to 2
- doc_lengths: int32 [4, 16], P('dp'), may hold values from 1 to 2048, 4096 in all within a row
- span_order: int32 [64], replicated, may hold values from 0 to 63, each once
Outputs:
- out: bfloat16 [4, 4096, 32, 128], P('dp', 'ctx', 'kvh')
- d_queries: bfloat16 [4, 4096, 32, 128], P('dp', 'ctx', 'kvh')
- d_keys: bfloat16 [4, 4096, 4, 128], P('dp', 'ctx', 'kvh')
- d_values: bfloat16 [4, 4096, 4, 128], P('dp', 'ctx', 'kvh')
- d_head_scale: float32 [32], replicated
Inputs may be any that keep to these rules, and one draw needn't show every extreme that they name: `doc_lengths`: each row sums to 4096; the longest document of each row reaches the maximum. `span_order`: each block number appears once.
All inputs are finite; a program needn't handle non-finite values.
Results may differ from a plain program's by a relative error of at most 0.03.
Values may be sent and summed in bfloat16 or wider, within the bound.
A program may use at most 64 MiB of HBM per device.

v0:
```python
import math

import jax
import jax.numpy as jnp
from jax import lax
from jax.sharding import PartitionSpec as P

masked_low = -1e30


def span_places(span_order, row_ids, span_rows):
    slot_ids = jnp.arange(span_order.shape[0], dtype=jnp.int32)
    picked = jnp.sum(
        jnp.where((row_ids // span_rows)[:, None] == slot_ids[None, :], span_order[None, :], 0),
        axis=1,
    )
    return picked * span_rows + row_ids % span_rows


def document_ids(doc_row, places):
    bounds = jnp.cumsum(doc_row)
    return jnp.sum((bounds[None, :] <= places[:, None]).astype(jnp.int32), axis=1)


def block_scores(queries, key_block, factor, query_info, key_place, key_doc):
    raw_dot = jnp.einsum("thd,sd->hts", queries, key_block, preferred_element_type=jnp.float32)
    visible = (query_info[1][:, None] == key_doc[None, :]) & (
        key_place[None, :] <= query_info[0][:, None]
    )
    return (raw_dot * factor[:, None, None], visible)


def absorb_totals(carry_state, queries, key_block, factor, query_info, key_place, key_doc):
    row_peak, row_total = carry_state
    scores, visible = block_scores(queries, key_block, factor, query_info, key_place, key_doc)
    masked = jnp.where(visible[None], scores, masked_low)
    new_peak = jnp.maximum(row_peak, jnp.max(masked, axis=2))
    weights = jnp.where(visible[None], jnp.exp(masked - new_peak[:, :, None]), 0.0)
    row_total = row_total * jnp.exp(row_peak - new_peak) + jnp.sum(weights, axis=2)
    return (new_peak, row_total)


def add_output(
    out_accum, queries, key_block, value_block, factor, query_info, key_place, key_doc, norm_log
):
    scores, visible = block_scores(queries, key_block, factor, query_info, key_place, key_doc)
    prob_bf = jnp.where(visible[None], jnp.exp(scores - norm_log[:, :, None]), 0.0).astype(
        jnp.bfloat16
    )
    return out_accum + jnp.einsum(
        "hts,sd->thd", prob_bf, value_block, preferred_element_type=jnp.float32
    )


def block_grads(
    queries, d_rows, key_block, value_block, factor, query_info, key_place, key_doc, norm_log, delta
):
    scores, visible = block_scores(queries, key_block, factor, query_info, key_place, key_doc)
    centred = jnp.where(visible[None], scores - norm_log[:, :, None], 0.0)
    prob_bf = jnp.where(visible[None], jnp.exp(centred), 0.0).astype(jnp.bfloat16)
    d_prob = jnp.einsum("thd,sd->hts", d_rows, value_block, preferred_element_type=jnp.float32)
    d_score = (prob_bf.astype(jnp.float32) * (d_prob - delta[:, :, None])).astype(jnp.bfloat16)
    scale_part = jnp.sum(d_score.astype(jnp.float32) * centred, axis=(1, 2))
    d_query = jnp.einsum("hts,sd->thd", d_score, key_block, preferred_element_type=jnp.float32)
    head_keys = jnp.einsum("hts,thd->hsd", d_score, queries, preferred_element_type=jnp.float32)
    d_key = jnp.sum(head_keys * factor[:, None, None], axis=0)
    d_value = jnp.einsum("hts,thd->sd", prob_bf, d_rows, preferred_element_type=jnp.float32)
    return (d_query, d_key, d_value, scale_part)


def local(queries, keys, values, d_out, head_scale, doc_lengths, span_order):
    query_rows = queries[0]
    d_rows = d_out[0]
    key_rows = keys[0, :, 0, :]
    value_rows = values[0, :, 0, :]
    tok_rows = query_rows.shape[0]
    group_size = query_rows.shape[1]
    head_size = query_rows.shape[2]
    span_rows = tok_rows // 2
    ctx_count = lax.axis_size("ctx")
    ctx_index = lax.axis_index("ctx")
    total_rows = tok_rows * ctx_count
    key_places = span_places(span_order, jnp.arange(total_rows, dtype=jnp.int32), span_rows)
    key_docs = document_ids(doc_lengths[0], key_places)
    query_info = (
        lax.dynamic_slice_in_dim(key_places, ctx_index * tok_rows, tok_rows),
        lax.dynamic_slice_in_dim(key_docs, ctx_index * tok_rows, tok_rows),
    )
    head_start = lax.axis_index("kvh") * group_size
    scales = lax.dynamic_slice_in_dim(head_scale, head_start, group_size)
    factor = scales / math.sqrt(head_size)
    start_state = (
        jnp.full((group_size, tok_rows), masked_low, jnp.float32),
        jnp.zeros((group_size, tok_rows), jnp.float32),
    )
    zero_query = jnp.zeros((tok_rows, group_size, head_size), jnp.float32)
    zero_scale = jnp.zeros((group_size,), jnp.float32)
    gathered_keys, gathered_values = (
        lax.all_gather(key_rows, "ctx", axis=0, tiled=True),
        lax.all_gather(value_rows, "ctx", axis=0, tiled=True),
    )
    shard_group = max(1, min(ctx_count, 512 // tok_rows))
    block_count = ctx_count // shard_group
    block_rows = tok_rows * shard_group
    key_blocks = (
        gathered_keys.reshape(block_count, block_rows, head_size),
        gathered_values.reshape(block_count, block_rows, head_size),
        key_places.reshape(block_count, block_rows),
        key_docs.reshape(block_count, block_rows),
    )

    def totals_step(carry_state, pieces):
        return (
            absorb_totals(
                carry_state, query_rows, pieces[0], factor, query_info, pieces[2], pieces[3]
            ),
            None,
        )

    row_peak, row_total = lax.scan(totals_step, start_state, key_blocks)[0]
    norm_log = row_peak + jnp.log(row_total)

    def output_step(out_accum, pieces):
        return (
            add_output(
                out_accum,
                query_rows,
                pieces[0],
                pieces[1],
                factor,
                query_info,
                pieces[2],
                pieces[3],
                norm_log,
            ),
            None,
        )

    out_accum = lax.scan(output_step, zero_query, key_blocks)[0]
    out_bf = out_accum.astype(jnp.bfloat16)
    delta = jnp.sum(d_rows.astype(jnp.float32) * out_bf.astype(jnp.float32), axis=2).T

    def backward_step(carried, pieces):
        d_query, scale_accum = carried
        dq_part, dk_part, dv_part, scale_part = block_grads(
            query_rows,
            d_rows,
            pieces[0],
            pieces[1],
            factor,
            query_info,
            pieces[2],
            pieces[3],
            norm_log,
            delta,
        )
        return ((d_query + dq_part, scale_accum + scale_part), (dk_part, dv_part))

    (d_query, scale_accum), (dk_terms, dv_terms) = lax.scan(
        backward_step, (zero_query, zero_scale), key_blocks
    )
    d_key_rows, d_value_rows = (
        lax.psum_scatter(
            dk_terms.reshape(total_rows, head_size), "ctx", scatter_dimension=0, tiled=True
        ),
        lax.psum_scatter(
            dv_terms.reshape(total_rows, head_size), "ctx", scatter_dimension=0, tiled=True
        ),
    )
    dq_full = d_query * factor[None, :, None]
    scale_terms = scale_accum / scales
    placed = lax.dynamic_update_slice_in_dim(
        jnp.zeros((head_scale.shape[0],), jnp.float32), scale_terms, head_start, 0
    )
    d_head_scale = lax.psum(placed, ("ctx", "kvh", "dp"))
    return (
        out_bf[None],
        dq_full.astype(jnp.bfloat16)[None],
        d_key_rows.astype(jnp.bfloat16)[None, :, None, :],
        d_value_rows.astype(jnp.bfloat16)[None, :, None, :],
        d_head_scale,
    )


def solution(mesh):
    return jax.shard_map(
        local,
        mesh=mesh,
        in_specs=(
            P("dp", "ctx", "kvh", None),
            P("dp", "ctx", "kvh", None),
            P("dp", "ctx", "kvh", None),
            P("dp", "ctx", "kvh", None),
            P(),
            P("dp", None),
            P(),
        ),
        out_specs=(
            P("dp", "ctx", "kvh", None),
            P("dp", "ctx", "kvh", None),
            P("dp", "ctx", "kvh", None),
            P("dp", "ctx", "kvh", None),
            P(),
        ),
        check_vma=False,
    )
```

profile of v0, /device:TPU:16, one launch (start us, length us, event | category | flops | bytes accessed | tf_op | source)
XLA Modules:
  0.0 1029.4 jit_solution(1651963688542715615)
XLA Ops:
  11.9 1.7 copy.47
  14.3 222.2 %all-gather.7.cloned.1.call-done = bf16[1,4096,1,128]{3,1,2,0:T(8,128)(2,1)} async-done(((bf16[1,128,1,128]{3,1,2,0:T(8,128)(2,1)}), bf16[1,4096,1,128]{3,1,2,0:T(8,128)(2,1)}) %all-gather.7.cloned.1.call-update) | async-done | bytes 1048592 | tf_op jit(solution)/shard_map/all_gather | solution.py:99
  236.4 17.8 %while.41 = (s32[]{:T(128)}, f32[8,128]{1,0:T(8,128)S(1)}, f32[8,128]{1,0:T(8,128)S(1)}, s32[128]{0:T(128)S(1)}, s32[8,512]{1,0:T(8,128)S(1)}, /*index=5*/s32[8,...) while((s32[]{:T(128)}, f32[8,128]{1,0:T(8,128)S(1)}, ...), condition=%wide.region_6.7_spmd.clone, body=%wide.region_3.6_spmd.clone.sunk | while | flops 138613760 | bytes 4850896 | solution.py:120
  236.7 1.4 fusion.80
  241.1 1.4 fusion.80
  245.6 1.4 fusion.80
  250.0 1.4 fusion.80
  252.3 1.4 fusion.80
  254.3 204.3 %all-gather.5.cloned.1.call-done = bf16[1,4096,1,128]{3,1,2,0:T(8,128)(2,1)} async-done(((bf16[1,128,1,128]{3,1,2,0:T(8,128)(2,1)}), bf16[1,4096,1,128]{3,1,2,0:T(8,128)(2,1)}) %all-gather.5.cloned.1.call-update) | async-done | bytes 1048592 | tf_op jit(solution)/shard_map/all_gather | solution.py:100
  458.6 15.7 %while.42 = (s32[]{:T(128)}, f32[128,8,128]{0,2,1:T(8,128)S(1)}, bf16[8,512,128]{2,1,0:T(8,128)(2,1)}, s32[128]{0:T(128)S(1)}, s32[8,512]{1,0:T(8,128)S(1)}, /*i...) while((s32[]{:T(128)}, f32[128,8,128]{0,2,1:T(8,128)S(1)}, ...), condition=%wide.region_8.9_spmd.clone, body=%wide.region_7.8_spmd.clone.sunk | while | flops 270991360 | bytes 1723058 | solution.py:139
  458.9 1.7 fusion.85
  460.8 1.7 fusion.85
  462.8 1.7 fusion.85
  464.8 1.7 fusion.85
  466.7 1.7 fusion.85
  468.7 1.7 fusion.85
  470.7 1.7 fusion.85
  472.6 1.7 fusion.85
  475.3 66.9 %while.43 = (s32[]{:T(128)}, f32[128,8,128]{0,2,1:T(8,128)}, f32[8]{0:T(128)S(1)}, f32[8,512,128]{2,1,0:T(8,128)}, f32[8,512,128]{2,1,0:T(8,128)}, /*index=5*/bf...) while((s32[]{:T(128)}, f32[128,8,128]{0,2,1:T(8,128)}, ...), condition=%wide.region_13.14_spmd.clone, body=%wide.region_10.13_spmd.clone.sunk | while | flops 681443328 | bytes 15295976 | solution.py:159
  475.3 1.4 fusion.94
  477.0 2.0 multiply_reduce_fusion.5
  478.9 2.1 fusion.95
  483.5 1.4 fusion.94
  485.2 2.0 multiply_reduce_fusion.5
  487.1 2.3 fusion.95
  491.9 1.4 fusion.94
  493.5 2.0 multiply_reduce_fusion.5
  495.5 2.3 fusion.95
  500.3 1.4 fusion.94
  501.9 2.0 multiply_reduce_fusion.5
  503.9 2.3 fusion.95
  508.7 1.4 fusion.94
  510.3 2.0 multiply_reduce_fusion.5
  512.3 2.3 fusion.95
  517.1 1.4 fusion.94
  518.7 2.0 multiply_reduce_fusion.5
  520.7 2.3 fusion.95
  525.5 1.4 fusion.94
  527.1 2.0 multiply_reduce_fusion.5
  529.1 2.3 fusion.95
  533.9 1.4 fusion.94
  535.5 2.0 multiply_reduce_fusion.5
  537.4 2.3 fusion.95
  543.1 100.8 %psum.7 = f32[32]{0:T(128)} all-reduce(f32[32]{0:T(128)S(1)} %divide_dynamic-update-slice_fusion), channel_id=1, replica_groups=mesh['ctx'=32,'kvh'=4,'dp'=4] {'ctx','kvh','dp'}, use_global_device_ids=true, to_apply=%region_16.17 | all-reduce | flops 32 | bytes 256 | tf_op jit(solution)/shard_map/psum | solution.py:175
  644.9 139.0 %reduce-scatter.3.cloned.1.call-done = f32[128,128]{1,0:T(8,128)} async-done(((f32[4096,128]{1,0:T(8,128)}), f32[128,128]{1,0:T(8,128)}) %reduce-scatter.3.cloned.1.call-update) | async-done | bytes 65552 | tf_op jit(solution)/shard_map/reduce_scatter | solution.py:163
  783.9 1.5 convert_bitcast_fusion.2
  785.4 236.1 %reduce-scatter.5.cloned.1.call-done = f32[128,128]{1,0:T(8,128)} async-done(((f32[4096,128]{1,0:T(8,128)}), f32[128,128]{1,0:T(8,128)}) %reduce-scatter.5.cloned.1.call-update) | async-done | bytes 65552 | tf_op jit(solution)/shard_map/reduce_scatter | solution.py:166
  1021.4 1.5 convert_bitcast_fusion.1
  (192 shorter events, 42.0 us)
Async XLA Ops:
  7.2 229.3 %all-gather.7.cloned.1.call-start = ((), (), s32[]{:S(2)}) async-start(), calls=%async_computation.5 | async-start | bytes 1081344 | tf_op jit(solution)/shard_map/all_gather | solution.py:99
  7.9 450.7 %all-gather.5.cloned.1.call-start = ((), (), s32[]{:S(2)}) async-start(), calls=%async_computation.4 | async-start | bytes 1081344 | tf_op jit(solution)/shard_map/all_gather | solution.py:100
  8.6 775.2 %reduce-scatter.3.cloned.1.call-start = ((), (), s32[]{:S(2)}) async-start(), calls=%async_computation.2 | async-start | bytes 2162688 | tf_op jit(solution)/shard_map/reduce_scatter | solution.py:163
  458.6 16.0 %copy-start.2 = (bf16[1,128,8,128]{3,2,1,0:T(8,128)(2,1)S(1)}, bf16[1,128,8,128]{3,2,1,0:T(8,128)(2,1)}, u32[]{:S(2)}) copy-start(bf16[1,128,8,128]{3,2,1,0:T(8,128)(2,1)} %param.16) | copy-start | bytes 786436
  474.6 0.7 copy-start.1
  475.3 1.6 copy-start.3
  478.9 3.3 copy-start.4
  483.5 1.6 copy-start.3
  487.1 3.5 copy-start.4
  491.9 1.6 copy-start.3
  495.5 3.5 copy-start.4
  500.3 1.6 copy-start.3
  503.9 3.5 copy-start.4
  508.7 1.6 copy-start.3
  512.3 3.5 copy-start.4
  517.1 1.6 copy-start.3
  520.7 3.5 copy-start.4
  525.5 1.6 copy-start.3
  529.1 3.5 copy-start.4
  533.9 1.6 copy-start.3
  537.4 3.5 copy-start.4
  542.3 0.7 copy-start.5
  542.3 101.6 %copy-start = (f32[128,8,128]{0,2,1:T(8,128)S(1)}, f32[128,8,128]{0,2,1:T(8,128)}, u32[]{:S(2)}) copy-start(f32[128,8,128]{0,2,1:T(8,128)} %get-tuple-element.203) | copy-start | bytes 1572868
  542.3 479.1 %reduce-scatter.5.cloned.1.call-start = ((), (), s32[]{:S(2)}) async-start(), calls=%async_computation.3 | async-start | bytes 2162688 | tf_op jit(solution)/shard_map/reduce_scatter | solution.py:166
Sparse Core Ops, SparseCore 0:
  10.1 226.3 all-gather.6
  238.5 220.0 all-gather.4
  542.4 241.4 reduce-scatter.2
  786.8 234.5 reduce-scatter.4
where the time goes:
time: 1030 us
  waiting for transfers between devices  803 us (78%)
  blocking collectives  101 us (10%)
  matrix products  83.4 us (8%)
  other arithmetic  15.7 us (2%)
  between operations  13.9 us (1%)
  local copies, waits for them, and re-layouts  10.8 us (1%)
    reduce_scatter x1, waiting for transfers between devices, local(): lax.psum_scatter(dv_terms.reshape(total_rows, head_size), 'ctx', scatter_...  236 us
    all_gather x1, waiting for transfers between devices, local(): lax.all_gather(key_rows, 'ctx', axis=0, tiled=True)  222 us
    all_gather x1, waiting for transfers between devices, local(): lax.all_gather(value_rows, 'ctx', axis=0, tiled=True)  204 us
    reduce_scatter x1, waiting for transfers between devices, local(): lax.psum_scatter(dk_terms.reshape(total_rows, head_size), 'ctx', scatter_...  139 us
    psum x1, blocking collectives, local(): d_head_scale = lax.psum(placed, ('ctx', 'kvh', 'dp'))  101 us
    dot_general x16, matrix products, block_scores(): jnp.einsum('thd,sd->hts', queries, key_block, preferred_element_type=jnp....  21.9 us
  transfers between devices with their start and end apart: 4, of which 4 were waited for; matrix products, arithmetic and copies ran while one was open for 2% of the time, Pallas kernels for 0%

commit v1 on v0

v1 whole, which is shorter than its diff:
```python
import functools
import math

import jax
import jax.numpy as jnp
from jax import lax
from jax.experimental import pallas as pl
from jax.experimental.pallas import tpu as pltpu
from jax.sharding import PartitionSpec as P

MESH = pl.DeviceIdType.MESH
masked_low = -1e30
NX = 4
ROW_TILE = 256


def nt_dot(a, b):
    return lax.dot_general(a, b, (((1,), (1,)), ((), ())), preferred_element_type=jnp.float32)


def nn_dot(a, b):
    return lax.dot_general(a, b, (((1,), (0,)), ((), ())), preferred_element_type=jnp.float32)


def xor_index(a, b, count):
    total, bit = 0, 1
    while bit < count:
        total = total + ((a // bit + b // bit) % 2) * bit
        bit *= 2
    return total


def kernel(
    nz, group, tok, hd, docs,
    q_hbm, k_hbm, v_hbm, do_hbm, scale_ref, docs_ref, span_ref,
    out_hbm, dq_ref, dk_ref, dv_ref, hs_ref,
    q_s, do_s, qt_s, dot_s, kv, s_s, dp_s, row_lo, row_hi, m_s, l_s, acc_s,
    out_s, p_s, ds_s, part, rxa, rxc, rz,
    in_sem, g_recv, g_send, a_recv, a_send, c_recv, c_send, z_recv, z_send,
):
    rows = group * tok
    chunk = NX * tok
    span = tok // 2
    me = lax.axis_index("ctx")
    z, x = me // NX, me % NX
    xr, xl, xo = (x + 1) % NX, (x + 3) % NX, (x + 2) % NX
    dev_xr, dev_xl = z * NX + xr, z * NX + xl
    dev_zr, dev_zl = ((z + 1) % nz) * NX + x, ((z + nz - 1) % nz) * NX + x

    k_in = pltpu.make_async_copy(k_hbm, kv.at[me, 0], in_sem.at[0])
    v_in = pltpu.make_async_copy(v_hbm, kv.at[me, 1], in_sem.at[1])
    q_in = pltpu.make_async_copy(q_hbm, q_s, in_sem.at[2])
    do_in = pltpu.make_async_copy(do_hbm, do_s, in_sem.at[3])
    for load in (k_in, v_in, q_in, do_in):
        load.start()

    barrier = pltpu.get_barrier_semaphore()
    for neighbour in (dev_xr, dev_xl, dev_zr, dev_zl):
        pl.semaphore_signal(barrier, inc=1, device_id={"ctx": neighbour}, device_id_type=MESH)
    pl.semaphore_wait(barrier, 4)

    def remote(src, dst, send_sem, recv_sem, device):
        return pltpu.make_async_remote_copy(
            src_ref=src,
            dst_ref=dst,
            send_sem=send_sem,
            recv_sem=recv_sem,
            device_id={"ctx": device},
            device_id_type=MESH,
        )

    def z_copy(origin, side):
        slot = origin * NX + x
        return remote(
            kv.at[slot],
            kv.at[slot],
            g_send.at[side, origin],
            g_recv.at[slot, 0],
            dev_zr if side == 0 else dev_zl,
        )

    def x_copy(j, origin_x, side):
        zb = xor_index(z, j, nz)
        slot = zb * NX + origin_x
        return remote(
            kv.at[slot],
            kv.at[slot],
            g_send.at[2 + side, j],
            g_recv.at[slot, 0],
            dev_xr if side == 0 else dev_xl,
        )

    def relay_copy(j, origin_x, side):
        zb = xor_index(z, j, nz)
        slot = zb * NX + origin_x
        return remote(
            kv.at[slot, side],
            kv.at[slot, side],
            g_send.at[4 + side, j],
            g_recv.at[slot, side],
            dev_xr if side == 0 else dev_xl,
        )

    k_in.wait()
    v_in.wait()

    @pl.when(z < nz - 1)
    def _():
        z_copy(z, 0).start()

    @pl.when(z > 0)
    def _():
        z_copy(z, 1).start()

    x_copy(0, x, 0).start()
    x_copy(0, x, 1).start()

    head0 = lax.axis_index("kvh") * group
    sub = lax.broadcasted_iota(jnp.int32, (group, hd), 0)
    scale8 = jnp.zeros((group, hd), jnp.float32)
    for h in range(group):
        scale8 = jnp.where(sub == h, scale_ref[head0 + h], scale8)
    factor8 = scale8 * (1.0 / math.sqrt(hd))

    def per_row(tile8):
        count = ROW_TILE // group
        return jnp.broadcast_to(tile8[None], (count, group, hd)).reshape(ROW_TILE, hd)

    bounds = []
    running = jnp.int32(0)
    for d in range(docs):
        running = running + docs_ref[0, d]
        bounds.append(running)
    first_span, second_span = span_ref[2 * me], span_ref[2 * me + 1]

    def row_values(r, carry):
        base = r * ROW_TILE
        token = (lax.broadcasted_iota(jnp.int32, (ROW_TILE, hd), 0) + base) // group
        place = jnp.where(token < span, first_span * span, second_span * span - span) + token
        low = jnp.zeros_like(place)
        for bound in bounds:
            low = jnp.maximum(low, jnp.where(place >= bound, bound, 0))
        at = pl.ds(pl.multiple_of(base, ROW_TILE), ROW_TILE)
        row_hi[at] = place
        row_lo[at] = low
        m_s[at] = jnp.full((ROW_TILE, hd), masked_low, jnp.float32)
        l_s[at] = jnp.zeros((ROW_TILE, hd), jnp.float32)
        acc_s[at] = jnp.zeros((ROW_TILE, hd), jnp.float32)
        return carry

    lax.fori_loop(0, rows // ROW_TILE, row_values, 0)
    q_in.wait()
    do_in.wait()
    for r in range(rows // ROW_TILE):
        at = slice(r * ROW_TILE, (r + 1) * ROW_TILE)
        qt_s[:, at] = q_s[at].astype(jnp.float32).T.astype(jnp.bfloat16)
        dot_s[:, at] = do_s[at].astype(jnp.float32).T.astype(jnp.bfloat16)

    def chunk_rows(zb, which):
        return kv[pl.ds(zb * NX, NX), which].reshape(chunk, hd)

    def forward_chunk(j):
        zb = xor_index(z, j, nz)
        key_rows, value_rows = chunk_rows(zb, 0), chunk_rows(zb, 1)
        lane = lax.broadcasted_iota(jnp.int32, (group, tok), 1)
        places = []
        for b in range(NX):
            lower = span_ref[(zb * NX + b) * 2] * span
            upper = span_ref[(zb * NX + b) * 2 + 1] * span - span
            place = jnp.where(lane < span, lower, upper) + lane
            count = ROW_TILE // group
            places.append(jnp.broadcast_to(place[None], (count, group, tok)).reshape(ROW_TILE, tok))
        factor = per_row(factor8)
        for r in range(rows // ROW_TILE):
            at = slice(r * ROW_TILE, (r + 1) * ROW_TILE)
            raw = nt_dot(q_s[at], key_rows)
            low, high = row_lo[at], row_hi[at]
            scores = []
            for b in range(NX):
                visible = (places[b] >= low) & (places[b] <= high)
                score = jnp.where(visible, raw[:, b * tok : (b + 1) * tok] * factor, masked_low)
                s_s[j, at, b * tok : (b + 1) * tok] = score
                scores.append(score)
            peak = jnp.maximum(
                jnp.maximum(scores[0], scores[1]), jnp.maximum(scores[2], scores[3])
            )
            old = m_s[at]
            new = jnp.maximum(old, jnp.max(peak, axis=1, keepdims=True))
            m_s[at] = new
            alpha = jnp.exp(old - new)
            weights = [jnp.exp(score - new) for score in scores]
            l_s[at] = l_s[at] * alpha + ((weights[0] + weights[1]) + (weights[2] + weights[3]))
            weight_bf = jnp.concatenate([w.astype(jnp.bfloat16) for w in weights], axis=1)
            acc_s[at] = acc_s[at] * alpha + nn_dot(weight_bf, value_rows)
            d_prob = nt_dot(do_s[at], value_rows)
            for b in range(NX):
                dp_s[j, at, b * tok : (b + 1) * tok] = d_prob[:, b * tok : (b + 1) * tok] * factor

    def gather_step(i, carry):
        @pl.when(i < nz - 1)
        def _():
            d = i + 1

            @pl.when(z - d >= 0)
            def _():
                copy = z_copy(z - d, 0)
                copy.wait_recv()

                @pl.when(z < nz - 1)
                def _():
                    copy.start()

            @pl.when(z + d < nz)
            def _():
                copy = z_copy(z + d, 1)
                copy.wait_recv()

                @pl.when(z > 0)
                def _():
                    copy.start()

            x_copy(i + 1, x, 0).start()
            x_copy(i + 1, x, 1).start()

        @pl.when(i < nz)
        def _():
            x_copy(i, xl, 0).wait_recv()
            relay_copy(i, xl, 0).start()
            x_copy(i, xr, 1).wait_recv()
            relay_copy(i, xr, 1).start()

        @pl.when(i > 0)
        def _():
            relay_copy(i - 1, xo, 0).wait_recv()
            relay_copy(i - 1, xo, 1).wait_recv()
            forward_chunk(i - 1)

        return carry

    lax.fori_loop(0, nz + 1, gather_step, 0)

    def finish_rows(r, carry):
        at = pl.ds(pl.multiple_of(r * ROW_TILE, ROW_TILE), ROW_TILE)
        total = jnp.sum(l_s[at], axis=1, keepdims=True)
        out_rows = (acc_s[at] / total).astype(jnp.bfloat16)
        out_s[at] = out_rows
        m_s[at] = m_s[at] + jnp.log(total)
        product = do_s[at].astype(jnp.float32) * out_rows.astype(jnp.float32)
        l_s[at] = jnp.sum(product, axis=1, keepdims=True) * per_row(factor8)
        acc_s[at] = jnp.zeros((ROW_TILE, hd), jnp.float32)
        return carry

    lax.fori_loop(0, rows // ROW_TILE, finish_rows, 0)
    out_copy = pltpu.make_async_copy(out_s, out_hbm, in_sem.at[0])
    out_copy.start()

    def a_copy(j, side):
        return remote(
            part.at[j, xo, side],
            rxa.at[j, side],
            a_send.at[side, j],
            a_recv.at[side, j],
            dev_xl if side == 0 else dev_xr,
        )

    def c_copy(j, side):
        return remote(
            part.at[j, xl if side == 0 else xr],
            rxc.at[j, side],
            c_send.at[side, j],
            c_recv.at[side, j],
            dev_xl if side == 0 else dev_xr,
        )

    def z_sum_copy(j, zb, side):
        return remote(
            part.at[j, x],
            rz.at[side, zb],
            z_send.at[side, zb],
            z_recv.at[side, zb],
            dev_zr if side == 0 else dev_zl,
        )

    def add_bf(a, b):
        return (a.astype(jnp.float32) + b.astype(jnp.float32)).astype(jnp.bfloat16)

    hs_ref[...] = jnp.zeros_like(hs_ref)

    def backward_chunk(j):
        zb = xor_index(z, j, nz)
        key_rows = chunk_rows(zb, 0)
        hs_total = hs_ref[...]
        for r in range(rows // ROW_TILE):
            at = slice(r * ROW_TILE, (r + 1) * ROW_TILE)
            norm, delta = m_s[at], l_s[at]
            for b in range(NX):
                cols = slice(b * tok, (b + 1) * tok)
                centred = s_s[j, at, cols] - norm
                prob = jnp.exp(centred)
                d_score = prob * (dp_s[j, at, cols] - delta)
                p_s[at, cols] = prob.astype(jnp.bfloat16)
                ds_s[at, cols] = d_score.astype(jnp.bfloat16)
                terms = (d_score * centred).reshape(ROW_TILE // group, group, tok)
                hs_total = hs_total + jnp.sum(terms, axis=0)
            acc_s[at] = acc_s[at] + nn_dot(ds_s[at], key_rows)
        hs_ref[...] = hs_total
        d_key = nn_dot(qt_s[...], ds_s[...])
        d_value = nn_dot(dot_s[...], p_s[...])
        for b in range(NX):
            cols = slice(b * tok, (b + 1) * tok)
            part[j, b, 0] = d_key[:, cols].astype(jnp.bfloat16)
            part[j, b, 1] = d_value[:, cols].astype(jnp.bfloat16)

    def scatter_step(k, carry):
        @pl.when(k < nz)
        def _():
            j = nz - 1 - k
            backward_chunk(j)
            a_copy(j, 0).start()
            a_copy(j, 1).start()

        @pl.when((k >= 1) & (k <= nz))
        def _():
            j = nz - k
            a_copy(j, 0).wait_recv()
            part[j, xl, 0] = add_bf(part[j, xl, 0], rxa[j, 0])
            c_copy(j, 0).start()
            a_copy(j, 1).wait_recv()
            part[j, xr, 1] = add_bf(part[j, xr, 1], rxa[j, 1])
            c_copy(j, 1).start()

        @pl.when(k >= 2)
        def _():
            j = nz + 1 - k
            c_copy(j, 0).wait_recv()
            c_copy(j, 1).wait_recv()
            total = part[j, x].astype(jnp.float32) + rxc[j, 0].astype(jnp.float32)
            total = total + rxc[j, 1].astype(jnp.float32)
            part[j, x] = total.astype(jnp.bfloat16)

            @pl.when(j > 0)
            def _():
                @pl.when(z + j < nz)
                def _():
                    zb = z + j
                    at = xor_index(z, zb, nz)

                    @pl.when(z > 0)
                    def _():
                        z_sum_copy(at, zb, 0).wait_recv()
                        part[at, x] = add_bf(part[at, x], rz[0, zb])

                    z_sum_copy(at, zb, 0).start()

                @pl.when(z - j >= 0)
                def _():
                    zb = z - j
                    at = xor_index(z, zb, nz)

                    @pl.when(z < nz - 1)
                    def _():
                        z_sum_copy(at, zb, 1).wait_recv()
                        part[at, x] = add_bf(part[at, x], rz[1, zb])

                    z_sum_copy(at, zb, 1).start()

        return carry

    lax.fori_loop(0, nz + 2, scatter_step, 0)

    for r in range(rows // ROW_TILE):
        at = slice(r * ROW_TILE, (r + 1) * ROW_TILE)
        dq_ref[at] = acc_s[at].astype(jnp.bfloat16)

    @pl.when(z > 0)
    def _():
        z_sum_copy(0, z, 0).wait_recv()
        part[0, x] = add_bf(part[0, x], rz[0, z])

    @pl.when(z < nz - 1)
    def _():
        z_sum_copy(0, z, 1).wait_recv()
        part[0, x] = add_bf(part[0, x], rz[1, z])

    dk_ref[...] = part[0, x, 0].astype(jnp.float32).T.astype(jnp.bfloat16)
    dv_ref[...] = part[0, x, 1].astype(jnp.float32).T.astype(jnp.bfloat16)

    def drain(j, carry):
        x_copy(j, x, 0).wait_send()
        x_copy(j, x, 1).wait_send()
        relay_copy(j, xl, 0).wait_send()
        relay_copy(j, xr, 1).wait_send()
        a_copy(j, 0).wait_send()
        a_copy(j, 1).wait_send()
        c_copy(j, 0).wait_send()
        c_copy(j, 1).wait_send()

        @pl.when((j <= z) & (z < nz - 1))
        def _():
            z_copy(j, 0).wait_send()

        @pl.when((j >= z) & (z > 0))
        def _():
            z_copy(j, 1).wait_send()

        @pl.when(j > z)
        def _():
            z_sum_copy(xor_index(z, j, nz), j, 0).wait_send()

        @pl.when(j < z)
        def _():
            z_sum_copy(xor_index(z, j, nz), j, 1).wait_send()

        return carry

    lax.fori_loop(0, nz, drain, 0)
    out_copy.wait()


def local(queries, keys, values, d_out, head_scale, doc_lengths, span_order):
    _, tok, group, hd = queries.shape
    ctx = lax.axis_size("ctx")
    nz = ctx // NX
    rows, chunk = tok * group, NX * tok
    bf, f32, i32 = jnp.bfloat16, jnp.float32, jnp.int32
    any_spec = pl.BlockSpec(memory_space=pl.ANY)
    vmem_spec = pl.BlockSpec(memory_space=pltpu.VMEM)
    smem_spec = pl.BlockSpec(memory_space=pltpu.SMEM)
    dma = pltpu.SemaphoreType.DMA
    out, dq, dk, dv, hs = pl.pallas_call(
        functools.partial(kernel, nz, group, tok, hd, doc_lengths.shape[1]),
        out_shape=(
            jax.ShapeDtypeStruct((rows, hd), bf),
            jax.ShapeDtypeStruct((rows, hd), bf),
            jax.ShapeDtypeStruct((tok, hd), bf),
            jax.ShapeDtypeStruct((tok, hd), bf),
            jax.ShapeDtypeStruct((group, tok), f32),
        ),
        in_specs=[any_spec] * 4 + [smem_spec] * 3,
        out_specs=(any_spec, vmem_spec, vmem_spec, vmem_spec, vmem_spec),
        scratch_shapes=[
            pltpu.VMEM((rows, hd), bf),
            pltpu.VMEM((rows, hd), bf),
            pltpu.VMEM((hd, rows), bf),
            pltpu.VMEM((hd, rows), bf),
            pltpu.VMEM((ctx, 2, tok, hd), bf),
            pltpu.VMEM((nz, rows, chunk), f32),
            pltpu.VMEM((nz, rows, chunk), f32),
            pltpu.VMEM((rows, hd), i32),
            pltpu.VMEM((rows, hd), i32),
            pltpu.VMEM((rows, hd), f32),
            pltpu.VMEM((rows, hd), f32),
            pltpu.VMEM((rows, hd), f32),
            pltpu.VMEM((rows, hd), bf),
            pltpu.VMEM((rows, chunk), bf),
            pltpu.VMEM((rows, chunk), bf),
            pltpu.VMEM((nz, NX, 2, hd, tok), bf),
            pltpu.VMEM((nz, 2, hd, tok), bf),
            pltpu.VMEM((nz, 2, 2, hd, tok), bf),
            pltpu.VMEM((2, nz, 2, hd, tok), bf),
            dma((4,)),
            dma((ctx, 2)),
            dma((6, nz)),
            dma((2, nz)),
            dma((2, nz)),
            dma((2, nz)),
            dma((2, nz)),
            dma((2, nz)),
            dma((2, nz)),
        ],
        compiler_params=pltpu.CompilerParams(
            collective_id=0, has_side_effects=True, vmem_limit_bytes=60 * 1024 * 1024
        ),
    )(
        queries.reshape(rows, hd),
        keys.reshape(tok, hd),
        values.reshape(tok, hd),
        d_out.reshape(rows, hd),
        head_scale,
        doc_lengths,
        span_order,
    )
    head_start = lax.axis_index("kvh") * group
    scales = lax.dynamic_slice_in_dim(head_scale, head_start, group)
    scale_terms = jnp.sum(hs, axis=1) * math.sqrt(hd) / (scales * scales)
    placed = lax.dynamic_update_slice_in_dim(
        jnp.zeros((head_scale.shape[0],), f32), scale_terms, head_start, 0
    )
    d_head_scale = lax.psum(placed, ("ctx", "kvh", "dp"))
    return (
        out.reshape(queries.shape),
        dq.reshape(queries.shape),
        dk.reshape(keys.shape),
        dv.reshape(values.shape),
        d_head_scale,
    )


def solution(mesh):
    return jax.shard_map(
        local,
        mesh=mesh,
        in_specs=(
            P("dp", "ctx", "kvh", None),
            P("dp", "ctx", "kvh", None),
            P("dp", "ctx", "kvh", None),
            P("dp", "ctx", "kvh", None),
            P(),
            P("dp", None),
            P(),
        ),
        out_specs=(
            P("dp", "ctx", "kvh", None),
            P("dp", "ctx", "kvh", None),
            P("dp", "ctx", "kvh", None),
            P("dp", "ctx", "kvh", None),
            P(),
        ),
        check_vma=False,
    )
```

time: 1030 us -> 192 us (0.19)
  the two profiles are of different devices: /device:TPU:16 before, /device:TPU:1 now
where the time goes in v1:
time: 192 us; the launch traced here: 191 us
  blocking collectives  113 us (59%)
  Pallas kernels  72 us (38%)
  local copies, waits for them, and re-layouts  4.5 us (2%)
    psum x1, blocking collectives, local(): d_head_scale = lax.psum(placed, ('ctx', 'kvh', 'dp'))  113 us
    pallas_call x1, Pallas kernels, local(): pl.pallas_call(functools.partial(kernel, nz, group, tok, hd, doc_lengths....  72 us
    unnamed x12, local copies, waits for them, and re-layouts  4.5 us

profile of v1, /device:TPU:1, one launch (start us, length us, event | category | flops | bytes accessed | tf_op | source)
XLA Modules:
  0.0 191.5 jit_solution(13214582987192503000)
XLA Ops:
  0.6 72.0 %shard_map.110 = (bf16[1024,128]{1,0:T(8,128)(2,1)}, bf16[1024,128]{1,0:T(8,128)(2,1)}, bf16[128,128]{1,0:T(8,128)(2,1)}, bf16[128,128]{1,0:T(8,128)(2,1)}, f32[8,128]{1,0:T(8,128)}) custom-call(bf16[1024,128]{1,0:T(8,128)(2,1)} %bitcast.10, bf16[128,128]{1,0:T(8,128)(2,1)} %bitcast.14, bf16[128,128]{1,0:T(8,128)(2,1)} %bitcast.15, ...), custom_call_target="tpu_custom_call" | custom-call | tf_op jit(solution)/shard_map/pallas_call | solution.py:430
  72.6 0.8 reduce_sum.9
  73.5 0.0 copy-start.3
  73.5 0.6 copy-done.3
  74.1 0.2 divide_dynamic-update-slice_fusion
  74.3 113.3 %psum.7 = f32[32]{0:T(128)} all-reduce(f32[32]{0:T(128)S(1)} %divide_dynamic-update-slice_fusion), channel_id=1, replica_groups=mesh['ctx'=32,'kvh'=4,'dp'=4] {'ctx','kvh','dp'}, use_global_device_ids=true, to_apply=%region_1.0 | all-reduce | flops 32 | bytes 256 | tf_op jit(solution)/shard_map/psum | solution.py:489
  187.6 0.0 copy-start
  187.6 1.7 copy.17
  189.3 0.0 copy-done
  189.3 0.0 copy-start.2
  189.3 0.7 copy.18
  190.0 0.1 copy-done.2
  190.1 0.0 copy-start.1
  190.1 0.6 copy.19
  190.7 0.2 copy-done.1
  190.8 0.6 copy.20
  (1 shorter events, 0.0 us)
Async XLA Ops:
  73.5 0.7 copy-start.3
  187.6 1.7 copy-start
  189.3 0.8 copy-start.2
  190.1 0.8 copy-start.1

commit v2 on v1

v2 whole, which is shorter than its diff:
```python
import functools
import math

import jax
import jax.numpy as jnp
from jax import lax
from jax.experimental import pallas as pl
from jax.experimental.pallas import tpu as pltpu
from jax.sharding import PartitionSpec as P

MESH = pl.DeviceIdType.MESH
masked_low = -1e30
NX = 4
X_LAG = 2


def nt_dot(a, b):
    return lax.dot_general(a, b, (((1,), (1,)), ((), ())), preferred_element_type=jnp.float32)


def nn_dot(a, b):
    return lax.dot_general(a, b, (((1,), (0,)), ((), ())), preferred_element_type=jnp.float32)


def xor_index(a, b, count):
    total, bit = 0, 1
    while bit < count:
        total = total + (lax.rem(lax.div(a, bit) + lax.div(b, bit), 2)) * bit
        bit *= 2
    return total


def kernel(
    group, tok, hd, docs, nk, nd,
    q_hbm, k_hbm, v_hbm, do_hbm, scale_ref, docs_ref, span_ref,
    out_hbm, dq_hbm, dk_ref, dv_ref, hs_ref,
    q_s, do_s, qt_s, dot_s, kv, s_s, dp_s, row_lo, row_hi, m_s, l_s, acc_s,
    out_s, dq_s, p_s, ds_s, part, rxa, rxc, rz, hx, hz, hd_s,
    in_sem, g_recv, gz_send, gx_send, gr_send, a_send, a_recv,
    c_send, c_recv, z_send, z_recv,
    hx_send, hx_recv, hz_send, hz_recv, hd_send, hd_recv,
):
    nz = lax.axis_size("ctx") // NX
    rows = group * tok
    chunk = NX * tok
    span = tok // 2
    tile = min(512, rows)
    tiles = rows // tile
    me = lax.axis_index("ctx")
    ki, di = lax.axis_index("kvh"), lax.axis_index("dp")
    z, x = lax.div(me, NX), lax.rem(me, NX)
    pair = lax.div(z, 2)
    zp = z + 1 - 2 * lax.rem(z, 2)
    xr, xl, xo = lax.rem(x + 1, NX), lax.rem(x + 3, NX), lax.rem(x + 2, NX)

    def row(j):
        return xor_index(z, jnp.int32(j), nz)

    def z_dev(j):
        return {"ctx": row(j) * NX + x}

    def x_dev(shift):
        return {"ctx": z * NX + lax.rem(x + shift, NX)}

    right, left = x_dev(1), x_dev(3)
    mate = {"ctx": zp * NX + x}
    up = {"ctx": lax.rem(z + 2, nz) * NX + x}
    down = {"ctx": lax.rem(z + nz - 2, nz) * NX + x}

    def far_dev(t):
        return {"kvh": (ki + t // nd) % nk, "dp": (di + t % nd) % nd}

    k_in = pltpu.make_async_copy(k_hbm, kv.at[z, x, 0], in_sem.at[0])
    v_in = pltpu.make_async_copy(v_hbm, kv.at[z, x, 1], in_sem.at[1])
    q_in = pltpu.make_async_copy(q_hbm, q_s, in_sem.at[2])
    do_in = pltpu.make_async_copy(do_hbm, do_s, in_sem.at[3])
    for load in (k_in, v_in, q_in, do_in):
        load.start()

    barrier = pltpu.get_barrier_semaphore()
    partners = [z_dev(j) for j in range(1, nz)] + [x_dev(s) for s in range(1, NX)]
    partners = partners + [far_dev(t) for t in range(1, nk * nd)]
    for partner in partners:
        pl.semaphore_signal(barrier, inc=1, device_id=partner, device_id_type=MESH)
    pl.semaphore_wait(barrier, len(partners))

    def remote(src, dst, send_sem, recv_sem, device):
        return pltpu.make_async_remote_copy(
            src_ref=src,
            dst_ref=dst,
            send_sem=send_sem,
            recv_sem=recv_sem,
            device_id=device,
            device_id_type=MESH,
        )

    def block_copy(at, send_sem, device):
        return remote(kv.at[at], kv.at[at], send_sem, g_recv.at[at[0], at[1], 0], device)

    def line_copy(origin, side):
        return block_copy((origin, x), gz_send.at[side, origin], up if side == 0 else down)

    def mate_copy(origin):
        return block_copy((origin, x), gz_send.at[2, origin], mate)

    def x_copy(zb, bx, side):
        return block_copy((zb, bx), gx_send.at[side, zb], right if side == 0 else left)

    def relay_copy(zb, bx, side):
        at = (zb, bx, side)
        return remote(
            kv.at[at], kv.at[at], gr_send.at[side, zb], g_recv.at[at], right if side == 0 else left
        )

    def x_sends(zb):
        x_copy(zb, x, 0).start()
        x_copy(zb, x, 1).start()

    def relays(zb):
        x_copy(zb, xl, 0).wait_recv()
        relay_copy(zb, xl, 0).start()
        x_copy(zb, xr, 1).wait_recv()
        relay_copy(zb, xr, 1).start()

    def row_waits(zb):
        relay_copy(zb, xo, 0).wait_recv()
        relay_copy(zb, xo, 1).wait_recv()

    def forward_line(origin, side):
        @pl.when((z < nz - 2) if side == 0 else (z >= 2))
        def _():
            line_copy(origin, side).start()

    def line_step(e):
        if e < nz // 2:

            @pl.when(z >= 2 * e)
            def _():
                line_copy(z - 2 * e, 0).wait_recv()
                forward_line(z - 2 * e, 0)
                mate_copy(z - 2 * e).start()

            @pl.when(z + 2 * e < nz)
            def _():
                line_copy(z + 2 * e, 1).wait_recv()
                forward_line(z + 2 * e, 1)
                mate_copy(z + 2 * e).start()

        if e == 1:
            mate_copy(zp).wait_recv()
        else:

            @pl.when(zp >= 2 * (e - 1))
            def _():
                mate_copy(zp - 2 * (e - 1)).wait_recv()

            @pl.when(zp + 2 * (e - 1) < nz)
            def _():
                mate_copy(zp + 2 * (e - 1)).wait_recv()

    k_in.wait()
    v_in.wait()
    forward_line(z, 0)
    forward_line(z, 1)
    mate_copy(z).start()
    x_sends(z)

    head0 = ki * group
    sub = lax.broadcasted_iota(jnp.int32, (group, hd), 0)
    scale8 = jnp.zeros((group, hd), jnp.float32)
    for h in range(group):
        scale8 = jnp.where(sub == h, scale_ref[head0 + h], scale8)
    factor8 = scale8 * (1.0 / math.sqrt(hd))

    def per_row(tile8):
        return jnp.broadcast_to(tile8[None], (tile // group, group, hd)).reshape(tile, hd)

    bounds = []
    running = jnp.int32(0)
    for d in range(docs):
        running = running + docs_ref[0, d]
        bounds.append(running)
    first_span, second_span = span_ref[2 * me], span_ref[2 * me + 1]

    def row_values(r, carry):
        base = r * tile
        token = (lax.broadcasted_iota(jnp.int32, (tile, hd), 0) + base) // group
        place = jnp.where(token < span, first_span * span, second_span * span - span) + token
        low = jnp.zeros_like(place)
        for bound in bounds:
            low = jnp.maximum(low, jnp.where(place >= bound, bound, 0))
        at = pl.ds(pl.multiple_of(base, tile), tile)
        row_hi[at] = place
        row_lo[at] = low
        m_s[at] = jnp.full((tile, hd), masked_low, jnp.float32)
        l_s[at] = jnp.zeros((tile, hd), jnp.float32)
        acc_s[at] = jnp.zeros((tile, hd), jnp.float32)
        return carry

    lax.fori_loop(0, tiles, row_values, 0)
    q_in.wait()
    do_in.wait()

    def chunk_rows(zb, which):
        return kv[zb, :, which].reshape(chunk, hd)

    def forward_chunk(i, zb):
        key_rows, value_rows = chunk_rows(zb, 0), chunk_rows(zb, 1)
        lane = lax.broadcasted_iota(jnp.int32, (group, tok), 1)
        places = []
        for b in range(NX):
            owner = zb * NX + b
            lower = span_ref[owner * 2] * span
            upper = span_ref[owner * 2 + 1] * span - span
            place = jnp.where(lane < span, lower, upper) + lane
            places.append(
                jnp.broadcast_to(place[None], (tile // group, group, tok)).reshape(tile, tok)
            )
        factor = per_row(factor8)
        for r in range(tiles):
            at = slice(r * tile, (r + 1) * tile)
            raw = nt_dot(q_s[at], key_rows)
            low, high = row_lo[at], row_hi[at]
            scores = []
            for b in range(NX):
                visible = (places[b] >= low) & (places[b] <= high)
                score = jnp.where(visible, raw[:, b * tok : (b + 1) * tok] * factor, masked_low)
                s_s[i, at, b * tok : (b + 1) * tok] = score
                scores.append(score)
            peak = jnp.maximum(
                jnp.maximum(scores[0], scores[1]), jnp.maximum(scores[2], scores[3])
            )
            old = m_s[at]
            new = jnp.maximum(old, jnp.max(peak, axis=1, keepdims=True))
            m_s[at] = new
            alpha = jnp.exp(old - new)
            weights = [jnp.exp(score - new) for score in scores]
            l_s[at] = l_s[at] * alpha + ((weights[0] + weights[1]) + (weights[2] + weights[3]))
            for b in range(NX):
                p_s[at, b * tok : (b + 1) * tok] = weights[b].astype(jnp.bfloat16)
            acc_s[at] = acc_s[at] * alpha
            d_prob = nt_dot(do_s[at], value_rows)
            for b in range(NX):
                dp_s[i, at, b * tok : (b + 1) * tok] = d_prob[:, b * tok : (b + 1) * tok] * factor
        acc_s[...] = acc_s[...] + nn_dot(p_s[...], value_rows)

    def gather_step(i, carry):
        for e in range(1, nz // 2 + 1):

            @pl.when(i == 2 * e - 1)
            def _():
                line_step(e)

        @pl.when((i > 0) & (i < nz))
        def _():
            x_sends(row(i))

        @pl.when((i >= X_LAG) & (i < nz + X_LAG))
        def _():
            relays(row(i - X_LAG))

        @pl.when(i >= 2 * X_LAG)
        def _():
            zb = row(i - 2 * X_LAG)
            row_waits(zb)
            forward_chunk(i - 2 * X_LAG, zb)

        return carry

    lax.fori_loop(0, nz + 2 * X_LAG, gather_step, 0)

    def finish_rows(r, carry):
        at = pl.ds(pl.multiple_of(r * tile, tile), tile)
        total = jnp.sum(l_s[at], axis=1, keepdims=True)
        out_rows = (acc_s[at] / total).astype(jnp.bfloat16)
        out_s[at] = out_rows
        m_s[at] = m_s[at] + jnp.log(total)
        product = do_s[at].astype(jnp.float32) * out_rows.astype(jnp.float32)
        l_s[at] = jnp.sum(product, axis=1, keepdims=True) * per_row(factor8)
        acc_s[at] = jnp.zeros((tile, hd), jnp.float32)
        return carry

    lax.fori_loop(0, tiles, finish_rows, 0)
    out_copy = pltpu.make_async_copy(out_s, out_hbm, in_sem.at[0])
    out_copy.start()
    for r in range(tiles):
        at = slice(r * tile, (r + 1) * tile)
        qt_s[:, at] = q_s[at].astype(jnp.float32).T.astype(jnp.bfloat16)
        dot_s[:, at] = do_s[at].astype(jnp.float32).T.astype(jnp.bfloat16)

    def a_copy(j, side):
        return remote(
            part.at[j, xo, side],
            rxa.at[j, side],
            a_send.at[j, side],
            a_recv.at[j, side],
            left if side == 0 else right,
        )

    def c_copy(j, side, piece):
        return remote(
            part.at[j, xl if side == 0 else xr, piece],
            rxc.at[j, side, piece],
            c_send.at[j, side, piece],
            c_recv.at[j, side, piece],
            left if side == 0 else right,
        )

    def line_sum(j, zb, side):
        return remote(
            part.at[j, x], rz.at[side, zb], z_send.at[side, zb], z_recv.at[side, zb],
            up if side == 0 else down,
        )

    def mate_sum(j, zb):
        return remote(part.at[j, x], rz.at[2, zb], z_send.at[2, zb], z_recv.at[2, zb], mate)

    def add_bf(a, b):
        return (a.astype(jnp.float32) + b.astype(jnp.float32)).astype(jnp.bfloat16)

    def neighbour_sums(j):
        a_copy(j, 0).wait_recv()
        part[j, xl, 0] = add_bf(part[j, xl, 0], rxa[j, 0])
        c_copy(j, 0, 0).start()
        a_copy(j, 1).wait_recv()
        part[j, xr, 1] = add_bf(part[j, xr, 1], rxa[j, 1])
        c_copy(j, 1, 1).start()

    def column_sums(j):
        for side in range(2):
            for piece in range(2):
                c_copy(j, side, piece).wait_recv()
        total = part[j, x].astype(jnp.float32) + rxc[j, 0].astype(jnp.float32)
        total = total + rxc[j, 1].astype(jnp.float32)
        part[j, x] = total.astype(jnp.bfloat16)

    def to_mate(s):
        def send(target):
            mate_sum(2 * xor_index(pair, target, nz // 2) + 1, zp + 2 * (target - pair)).start()

        if s == 0:
            send(pair)
        else:

            @pl.when(pair + s < nz // 2)
            def _():
                send(pair + s)

            @pl.when(pair >= s)
            def _():
                send(pair - s)

    def along_line(s):
        @pl.when(pair + s < nz // 2)
        def _():
            zb = z + 2 * s
            at = 2 * xor_index(pair, pair + s, nz // 2)
            mate_sum(at, zb).wait_recv()
            part[at, x] = add_bf(part[at, x], rz[2, zb])

            @pl.when(pair > 0)
            def _():
                line_sum(at, zb, 0).wait_recv()
                part[at, x] = add_bf(part[at, x], rz[0, zb])

            line_sum(at, zb, 0).start()

        @pl.when(pair >= s)
        def _():
            zb = z - 2 * s
            at = 2 * xor_index(pair, pair - s, nz // 2)
            mate_sum(at, zb).wait_recv()
            part[at, x] = add_bf(part[at, x], rz[2, zb])

            @pl.when(pair < nz // 2 - 1)
            def _():
                line_sum(at, zb, 1).wait_recv()
                part[at, x] = add_bf(part[at, x], rz[1, zb])

            line_sum(at, zb, 1).start()

    hs_ref[...] = jnp.zeros_like(hs_ref)
    hx[x] = jnp.zeros((group, tok), jnp.float32)

    def backward_chunk(i):
        key_rows = chunk_rows(row(i), 0)
        hs_total = hx[x]
        for r in range(tiles):
            at = slice(r * tile, (r + 1) * tile)
            norm, delta = m_s[at], l_s[at]
            for b in range(NX):
                cols = slice(b * tok, (b + 1) * tok)
                centred = s_s[i, at, cols] - norm
                prob = jnp.exp(centred)
                d_score = prob * (dp_s[i, at, cols] - delta)
                p_s[at, cols] = prob.astype(jnp.bfloat16)
                ds_s[at, cols] = d_score.astype(jnp.bfloat16)
                terms = (d_score * centred).reshape(tile // group, group, tok)
                hs_total = hs_total + jnp.sum(terms, axis=0)
            acc_s[at] = acc_s[at] + nn_dot(ds_s[at], key_rows)
        hx[x] = hs_total
        d_key = nn_dot(qt_s[...], ds_s[...])
        d_value = nn_dot(dot_s[...], p_s[...])
        for b in range(NX):
            cols = slice(b * tok, (b + 1) * tok)
            part[i, b, 0] = d_key[:, cols].astype(jnp.bfloat16)
            part[i, b, 1] = d_value[:, cols].astype(jnp.bfloat16)

    def hx_copy(s):
        return remote(
            hx.at[x], hx.at[x], hx_send.at[s], hx_recv.at[x], x_dev(s)
        )

    def hz_copy(j):
        return remote(hz.at[z], hz.at[z], hz_send.at[j], hz_recv.at[z], z_dev(j))

    def far_copy(t):
        slot = ki * nd + di
        return remote(hd_s.at[slot], hd_s.at[slot], hd_send.at[t], hd_recv.at[slot], far_dev(t))

    def arrived(buffer, sems, slot):
        remote(buffer.at[slot], buffer.at[slot], sems.at[slot], sems.at[slot], x_dev(1)).wait_recv()

    def scatter_step(k, carry):
        @pl.when(k < nz)
        def _():
            j = nz - 1 - k
            backward_chunk(j)
            a_copy(j, 0).start()
            a_copy(j, 1).start()
            c_copy(j, 0, 1).start()
            c_copy(j, 1, 0).start()

        @pl.when(k == nz - 1)
        def _():
            for s in range(1, NX):
                hx_copy(s).start()
            for r in range(tiles):
                at = slice(r * tile, (r + 1) * tile)
                dq_s[at] = acc_s[at].astype(jnp.bfloat16)
            dq_copy.start()

        @pl.when((k >= X_LAG) & (k < nz + X_LAG))
        def _():
            neighbour_sums(nz - 1 - k + X_LAG)

        @pl.when(k >= 2 * X_LAG)
        def _():
            j = nz - 1 - k + 2 * X_LAG
            column_sums(j)

        for f in range(nz // 2):

            @pl.when(k == 2 * X_LAG + 2 * f)
            def _():
                if f > 0:
                    along_line(nz // 2 - f)
                to_mate(nz // 2 - 1 - f)

        @pl.when(k == nz)
        def _():
            for s in range(1, NX):
                arrived(hx, hx_recv, (x + s) % NX)
            hz[z] = (hx[0] + hx[1]) + (hx[2] + hx[3])
            for j in range(1, nz):
                hz_copy(j).start()

        @pl.when(k == nz + 2)
        def _():
            for j in range(1, nz):
                arrived(hz, hz_recv, row(j))
            hs_line = hz[0]
            for j in range(1, nz):
                hs_line = hs_line + hz[j]
            hd_s[ki * nd + di] = hs_line
            for t in range(1, nk * nd):
                far_copy(t).start()

        return carry

    dq_copy = pltpu.make_async_copy(dq_s, dq_hbm, in_sem.at[1])
    lax.fori_loop(0, nz + 2 * X_LAG, scatter_step, 0)

    total = part[0, x].astype(jnp.float32)
    mate_sum(0, z).wait_recv()
    rz_own = rz[2, z].astype(jnp.float32)
    part[0, x] = (total + rz_own).astype(jnp.bfloat16)

    @pl.when(pair > 0)
    def _():
        line_sum(0, z, 0).wait_recv()
        part[0, x] = add_bf(part[0, x], rz[0, z])

    @pl.when(pair < nz // 2 - 1)
    def _():
        line_sum(0, z, 1).wait_recv()
        part[0, x] = add_bf(part[0, x], rz[1, z])

    dk_ref[...] = part[0, x, 0].astype(jnp.float32).T.astype(jnp.bfloat16)
    dv_ref[...] = part[0, x, 1].astype(jnp.float32).T.astype(jnp.bfloat16)

    for t in range(1, nk * nd):
        arrived(hd_s, hd_recv, ((ki + t // nd) % nk) * nd + (di + t % nd) % nd)
    for kk in range(nk):
        head_total = hd_s[kk * nd]
        for dd in range(1, nd):
            head_total = head_total + hd_s[kk * nd + dd]
        hs_ref[kk * group : (kk + 1) * group] = head_total

    for s in range(1, NX):
        hx_copy(s).wait_send()
    for j in range(1, nz):
        hz_copy(j).wait_send()
    for t in range(1, nk * nd):
        far_copy(t).wait_send()

    def drain(j, carry):
        for side in range(2):
            x_copy(j, x, side).wait_send()
            relay_copy(j, xl, side).wait_send()
            a_copy(j, side).wait_send()
            for piece in range(2):
                c_copy(j, side, piece).wait_send()
        same = lax.rem(z + j, 2) == 0

        @pl.when(same)
        def _():
            mate_copy(j).wait_send()

            @pl.when((j <= z) & (z < nz - 2))
            def _():
                line_copy(j, 0).wait_send()

            @pl.when((j >= z) & (z >= 2))
            def _():
                line_copy(j, 1).wait_send()

            @pl.when(j > z)
            def _():
                line_sum(0, j, 0).wait_send()

            @pl.when(j < z)
            def _():
                line_sum(0, j, 1).wait_send()

        @pl.when(jnp.logical_not(same))
        def _():
            mate_sum(0, j).wait_send()

        return carry

    lax.fori_loop(0, nz, drain, 0)
    out_copy.wait()
    dq_copy.wait()


def local(queries, keys, values, d_out, head_scale, doc_lengths, span_order):
    _, tok, group, hd = queries.shape
    nz = lax.axis_size("ctx") // NX
    nk, nd = lax.axis_size("kvh"), lax.axis_size("dp")
    rows, chunk = tok * group, NX * tok
    bf, f32, i32 = jnp.bfloat16, jnp.float32, jnp.int32
    any_spec = pl.BlockSpec(memory_space=pl.ANY)
    vmem_spec = pl.BlockSpec(memory_space=pltpu.VMEM)
    smem_spec = pl.BlockSpec(memory_space=pltpu.SMEM)
    dma = pltpu.SemaphoreType.DMA
    out, dq, dk, dv, hs = pl.pallas_call(
        functools.partial(kernel, group, tok, hd, doc_lengths.shape[1], nk, nd),
        out_shape=(
            jax.ShapeDtypeStruct((rows, hd), bf),
            jax.ShapeDtypeStruct((rows, hd), bf),
            jax.ShapeDtypeStruct((tok, hd), bf),
            jax.ShapeDtypeStruct((tok, hd), bf),
            jax.ShapeDtypeStruct((nk * group, tok), f32),
        ),
        in_specs=[any_spec] * 4 + [smem_spec] * 3,
        out_specs=(any_spec, any_spec, vmem_spec, vmem_spec, vmem_spec),
        scratch_shapes=[
            pltpu.VMEM((rows, hd), bf),
            pltpu.VMEM((rows, hd), bf),
            pltpu.VMEM((hd, rows), bf),
            pltpu.VMEM((hd, rows), bf),
            pltpu.VMEM((nz, NX, 2, tok, hd), bf),
            pltpu.VMEM((nz, rows, chunk), f32),
            pltpu.VMEM((nz, rows, chunk), f32),
            pltpu.VMEM((rows, hd), i32),
            pltpu.VMEM((rows, hd), i32),
            pltpu.VMEM((rows, hd), f32),
            pltpu.VMEM((rows, hd), f32),
            pltpu.VMEM((rows, hd), f32),
            pltpu.VMEM((rows, hd), bf),
            pltpu.VMEM((rows, hd), bf),
            pltpu.VMEM((rows, chunk), bf),
            pltpu.VMEM((rows, chunk), bf),
            pltpu.VMEM((nz, NX, 2, hd, tok), bf),
            pltpu.VMEM((nz, 2, hd, tok), bf),
            pltpu.VMEM((nz, 2, 2, hd, tok), bf),
            pltpu.VMEM((3, nz, 2, hd, tok), bf),
            pltpu.VMEM((NX, group, tok), f32),
            pltpu.VMEM((nz, group, tok), f32),
            pltpu.VMEM((nk * nd, group, tok), f32),
            dma((4,)),
            dma((nz, NX, 2)),
            dma((3, nz)),
            dma((2, nz)),
            dma((2, nz)),
            dma((nz, 2)),
            dma((nz, 2)),
            dma((nz, 2, 2)),
            dma((nz, 2, 2)),
            dma((3, nz)),
            dma((3, nz)),
            dma((NX,)),
            dma((NX,)),
            dma((nz,)),
            dma((nz,)),
            dma((nk * nd,)),
            dma((nk * nd,)),
        ],
        compiler_params=pltpu.CompilerParams(
            collective_id=0, has_side_effects=True, vmem_limit_bytes=60 * 1024 * 1024
        ),
    )(
        queries.reshape(rows, hd),
        keys.reshape(tok, hd),
        values.reshape(tok, hd),
        d_out.reshape(rows, hd),
        head_scale,
        doc_lengths,
        span_order,
    )
    d_head_scale = jnp.sum(hs, axis=1) * math.sqrt(hd) / (head_scale * head_scale)
    return (
        out.reshape(queries.shape),
        dq.reshape(queries.shape),
        dk.reshape(keys.shape),
        dv.reshape(values.shape),
        d_head_scale,
    )


def solution(mesh):
    return jax.shard_map(
        local,
        mesh=mesh,
        in_specs=(
            P("dp", "ctx", "kvh", None),
            P("dp", "ctx", "kvh", None),
            P("dp", "ctx", "kvh", None),
            P("dp", "ctx", "kvh", None),
            P(),
            P("dp", None),
            P(),
        ),
        out_specs=(
            P("dp", "ctx", "kvh", None),
            P("dp", "ctx", "kvh", None),
            P("dp", "ctx", "kvh", None),
            P("dp", "ctx", "kvh", None),
            P(),
        ),
        check_vma=False,
    )
```

time: 192 us -> 95 us (0.49)
  blocking collectives: 113 us -> 0 us
  Pallas kernels: 72 us -> 88.3 us
    psum x1 -> x0, blocking collectives: 113 us -> none  [local(): d_head_scale = lax.psum(placed, ('ctx', 'kvh', 'dp'))]
    pallas_call x1, Pallas kernels: 72 us -> 88.3 us  [local(): pl.pallas_call(functools.partial(kernel, group, tok, hd, doc_lengths.shap...]
    unnamed x12 -> x14, local copies, waits for them, and re-layouts: 4.5 us -> 5.11 us
where the time goes in v2:
time: 95 us; the launch traced here: 94.7 us
  Pallas kernels  88.3 us (93%)
  local copies, waits for them, and re-layouts  5.11 us (5%)
    pallas_call x1, Pallas kernels, local(): pl.pallas_call(functools.partial(kernel, group, tok, hd, doc_lengths.shap...  88.3 us
    unnamed x14, local copies, waits for them, and re-layouts  5.11 us

profile of v2, /device:TPU:1, one launch (start us, length us, event | category | flops | bytes accessed | tf_op | source)
XLA Modules:
  0.0 94.7 jit_solution(1296649312715474340)
XLA Ops:
  0.6 88.3 %shard_map.110 = (bf16[1024,128]{1,0:T(8,128)(2,1)}, bf16[1024,128]{1,0:T(8,128)(2,1)}, bf16[128,128]{1,0:T(8,128)(2,1)}, bf16[128,128]{1,0:T(8,128)(2,1)}, f32[32,128]{1,0:T(8,128)}) custom-call(bf16[1024,128]{1,0:T(8,128)(2,1)} %bitcast.10, bf16[128,128]{1,0:T(8,128)(2,1)} %bitcast.14, bf16[128,128]{1,0:T(8,128)(2,1)} %bitcast.15, ...), custom_call_target="tpu_custom_call" | custom-call | tf_op jit(solution)/shard_map/pallas_call | solution.py:567
  88.9 0.0 copy-start.3
  88.9 0.7 copy-done.3
  89.6 0.0 copy-start.4
  89.6 0.1 reduce_sum.9
  89.8 0.5 copy-done.4
  90.3 0.5 multiply_divide_fusion
  90.8 0.0 copy-start
  90.8 1.7 %copy.16 = bf16[1,128,8,128]{3,2,1,0:T(8,128)(2,1)} copy(bf16[1,128,8,128]{3,2,1,0:T(8,128)(2,1)} %bitcast.9) | data formatting | bytes 524288
  92.5 0.0 copy-done
  92.5 0.0 copy-start.2
  92.5 0.7 copy.17
  93.2 0.1 copy-done.2
  93.3 0.0 copy-start.1
  93.3 0.6 copy.18
  93.9 0.2 copy-done.1
  94.1 0.6 copy.19
Async XLA Ops:
  88.9 0.7 copy-start.3
  89.6 0.7 copy-start.4
  90.8 1.7 %copy-start = (bf16[1024,128]{1,0:T(8,128)(2,1)S(1)}, bf16[1024,128]{1,0:T(8,128)(2,1)}, u32[]{:S(2)}) copy-start(bf16[1024,128]{1,0:T(8,128)(2,1)} %get-tuple-element.11) | copy-start | bytes 786436
  92.5 0.8 copy-start.2
  93.3 0.8 copy-start.1

commit v3 on v2

--- a/solution.py
+++ b/solution.py
@@ -34,11 +34,11 @@
     group, tok, hd, docs, nk, nd,
     q_hbm, k_hbm, v_hbm, do_hbm, scale_ref, docs_ref, span_ref,
     out_hbm, dq_hbm, dk_ref, dv_ref, hs_ref,
-    q_s, do_s, qt_s, dot_s, kv, s_s, dp_s, row_lo, row_hi, m_s, l_s, acc_s,
-    out_s, dq_s, p_s, ds_s, part, rxa, rxc, rz, hx, hz, hd_s,
+    q_s, do_s, qt_s, dot_s, kv, s_s, dp_s, row_lo, row_hi, m_s, l_s, wu_s, wd_s, wdu_s, acc_s,
+    out_s, dq_s, p_s, ds_s, part, rxa, rxc, rz, h_own, h_kv, h_plane, h_own_all, h_line, h_gate, h_hi, h_all,
     in_sem, g_recv, gz_send, gx_send, gr_send, a_send, a_recv,
     c_send, c_recv, z_send, z_recv,
-    hx_send, hx_recv, hz_send, hz_recv, hd_send, hd_recv,
+    h_send, hk_recv, hp_recv, hl_recv, hh_recv, ha_recv,
 ):
     nz = lax.axis_size("ctx") // NX
     rows = group * tok
@@ -56,9 +56,6 @@
     def row(j):
         return xor_index(z, jnp.int32(j), nz)
 
-    def z_dev(j):
-        return {"ctx": row(j) * NX + x}
-
     def x_dev(shift):
         return {"ctx": z * NX + lax.rem(x + shift, NX)}
 
@@ -67,8 +64,22 @@
     up = {"ctx": lax.rem(z + 2, nz) * NX + x}
     down = {"ctx": lax.rem(z + nz - 2, nz) * NX + x}
 
-    def far_dev(t):
-        return {"kvh": (ki + t // nd) % nk, "dp": (di + t % nd) % nd}
+    cores = min(2, nd)
+    core, hi = lax.rem(di, cores), lax.div(di, cores)
+    gate = (nz - 1) * (1 - hi)
+    at_gate = z == gate
+
+    def kv_dev(t):
+        return {"kvh": lax.rem(ki + t, nk)}
+
+    def plane_dev(t):
+        to_core = lax.rem(core + t // NX, cores)
+        return {"ctx": z * NX + lax.rem(x + t % NX, NX), "dp": hi * cores + to_core}
+
+    def line_dev(zz):
+        return {"ctx": zz * NX + x}
+
+    across = {"ctx": (nz - 1) * hi * NX + x, "dp": lax.rem(di + cores, nd)}
 
     k_in = pltpu.make_async_copy(k_hbm, kv.at[z, x, 0], in_sem.at[0])
     v_in = pltpu.make_async_copy(v_hbm, kv.at[z, x, 1], in_sem.at[1])
@@ -78,11 +89,32 @@
         load.start()
 
     barrier = pltpu.get_barrier_semaphore()
-    partners = [z_dev(j) for j in range(1, nz)] + [x_dev(s) for s in range(1, NX)]
-    partners = partners + [far_dev(t) for t in range(1, nk * nd)]
+    partners = [mate] + [kv_dev(t) for t in range(1, nk)]
+    partners = partners + [plane_dev(t) for t in range(1, NX * cores)]
+
+    def greet(partner):
+        pl.semaphore_signal(barrier, inc=1, device_id=partner, device_id_type=MESH)
+
     for partner in partners:
-        pl.semaphore_signal(barrier, inc=1, device_id=partner, device_id_type=MESH)
-    pl.semaphore_wait(barrier, len(partners))
+        greet(partner)
+
+    @pl.when(z < nz - 2)
+    def _():
+        greet(up)
+
+    @pl.when(z >= 2)
+    def _():
+        greet(down)
+
+    inner = jnp.where((z >= 2) & (z < nz - 2), 1, 0)
+    if nd > cores:
+
+        @pl.when(at_gate)
+        def _():
+            greet(across)
+
+        inner = inner + jnp.where(at_gate, 1, 0)
+    pl.semaphore_wait(barrier, len(partners) + 1 + inner)
 
     def remote(src, dst, send_sem, recv_sem, device):
         return pltpu.make_async_remote_copy(
@@ -193,8 +225,8 @@
         row_hi[at] = place
         row_lo[at] = low
         m_s[at] = jnp.full((tile, hd), masked_low, jnp.float32)
-        l_s[at] = jnp.zeros((tile, hd), jnp.float32)
-        acc_s[at] = jnp.zeros((tile, hd), jnp.float32)
+        for total in (l_s, wu_s, wd_s, wdu_s, acc_s):
+            total[at] = jnp.zeros((tile, hd), jnp.float32)
         return carry
 
     lax.fori_loop(0, tiles, row_values, 0)
@@ -233,15 +265,26 @@
             old = m_s[at]
             new = jnp.maximum(old, jnp.max(peak, axis=1, keepdims=True))
             m_s[at] = new
+            shift = new - old
             alpha = jnp.exp(old - new)
-            weights = [jnp.exp(score - new) for score in scores]
-            l_s[at] = l_s[at] * alpha + ((weights[0] + weights[1]) + (weights[2] + weights[3]))
+            d_prob = nt_dot(do_s[at], value_rows)
+            w_sum, wu_sum, wd_sum, wdu_sum = [jnp.zeros((tile, tok), jnp.float32)] * 4
             for b in range(NX):
-                p_s[at, b * tok : (b + 1) * tok] = weights[b].astype(jnp.bfloat16)
+                cols = slice(b * tok, (b + 1) * tok)
+                below = scores[b] - new
+                weight = jnp.exp(below)
+                d_scaled = d_prob[:, cols] * factor
+                p_s[at, cols] = weight.astype(jnp.bfloat16)
+                dp_s[i, at, cols] = d_scaled
+                weighted = weight * d_scaled
+                w_sum, wu_sum = w_sum + weight, wu_sum + weight * below
+                wd_sum, wdu_sum = wd_sum + weighted, wdu_sum + weighted * below
+            w_old, wd_old = l_s[at], wd_s[at]
+            wu_s[at] = alpha * (wu_s[at] - shift * w_old) + wu_sum
+            wdu_s[at] = alpha * (wdu_s[at] - shift * wd_old) + wdu_sum
+            l_s[at] = alpha * w_old + w_sum
+            wd_s[at] = alpha * wd_old + wd_sum
             acc_s[at] = acc_s[at] * alpha
-            d_prob = nt_dot(do_s[at], value_rows)
-            for b in range(NX):
-                dp_s[i, at, b * tok : (b + 1) * tok] = d_prob[:, b * tok : (b + 1) * tok] * factor
         acc_s[...] = acc_s[...] + nn_dot(p_s[...], value_rows)
 
     def gather_step(i, carry):
@@ -269,20 +312,99 @@
 
     lax.fori_loop(0, nz + 2 * X_LAG, gather_step, 0)
 
-    def finish_rows(r, carry):
+    def finish_rows(r, hs_total):
         at = pl.ds(pl.multiple_of(r * tile, tile), tile)
-        total = jnp.sum(l_s[at], axis=1, keepdims=True)
+        weights = l_s[at]
+        total = jnp.sum(weights, axis=1, keepdims=True)
+        log_total = jnp.log(total)
         out_rows = (acc_s[at] / total).astype(jnp.bfloat16)
         out_s[at] = out_rows
-        m_s[at] = m_s[at] + jnp.log(total)
+        m_s[at] = m_s[at] + log_total
         product = do_s[at].astype(jnp.float32) * out_rows.astype(jnp.float32)
-        l_s[at] = jnp.sum(product, axis=1, keepdims=True) * per_row(factor8)
+        delta = jnp.sum(product, axis=1, keepdims=True) * per_row(factor8)
+        terms = wdu_s[at] - delta * wu_s[at] - log_total * (wd_s[at] - delta * weights)
+        l_s[at] = delta
         acc_s[at] = jnp.zeros((tile, hd), jnp.float32)
-        return carry
-
-    lax.fori_loop(0, tiles, finish_rows, 0)
+        return hs_total + jnp.sum((terms / total).reshape(tile // group, group, hd), axis=0)
+
+    no_terms = jnp.zeros((group, hd), jnp.float32)
+    h_own[...] = lax.fori_loop(0, tiles, finish_rows, no_terms)
     out_copy = pltpu.make_async_copy(out_s, out_hbm, in_sem.at[0])
     out_copy.start()
+
+    def kv_share(t):
+        return remote(h_own, h_kv.at[ki], h_send.at[0, t], hk_recv.at[ki], kv_dev(t))
+
+    def plane_share(t):
+        slot = core * NX + x
+        return remote(h_kv, h_plane.at[slot], h_send.at[1, t], hp_recv.at[slot], plane_dev(t))
+
+    def line_share():
+        return remote(h_own_all, h_line.at[z], h_send.at[2, 0], hl_recv.at[z], line_dev(gate))
+
+    def across_share():
+        return remote(h_gate, h_hi.at[hi], h_send.at[3, 0], hh_recv.at[hi], across)
+
+    def all_share(zz):
+        return remote(h_all, h_all, h_send.at[4, zz], ha_recv.at[0], line_dev(zz))
+
+    def arrived(buffer, sem):
+        remote(buffer, buffer, sem, sem, right).wait_recv()
+
+    for t in range(1, nk):
+        kv_share(t).start()
+
+    def share_plane():
+        h_kv[ki] = h_own[...]
+        for t in range(1, nk):
+            slot = lax.rem(ki + t, nk)
+            arrived(h_kv.at[slot], hk_recv.at[slot])
+        for t in range(1, NX * cores):
+            plane_share(t).start()
+
+    def share_line():
+        h_plane[core * NX + x] = h_kv[...]
+        for t in range(1, NX * cores):
+            slot = lax.rem(core + t // NX, cores) * NX + lax.rem(x + t % NX, NX)
+            arrived(h_plane.at[slot], hp_recv.at[slot])
+        total = h_plane[0]
+        for t in range(1, NX * cores):
+            total = total + h_plane[t]
+        h_own_all[...] = total
+
+        @pl.when(jnp.logical_not(at_gate))
+        def _():
+            line_share().start()
+
+    def line_total():
+        h_line[z] = h_own_all[...]
+
+        def more(j, total):
+            zz = lax.rem(gate + j, nz)
+            arrived(h_line.at[zz], hl_recv.at[zz])
+            return total
+
+        lax.fori_loop(1, nz, more, 0)
+        total = h_line[0]
+        for zz in range(1, nz):
+            total = total + h_line[zz]
+        h_gate[...] = total
+
+    def share_across():
+        line_total()
+        if nd > cores:
+            across_share().start()
+
+    def share_all():
+        if nd > cores:
+            arrived(h_hi.at[1 - hi], hh_recv.at[1 - hi])
+            h_hi[hi] = h_gate[...]
+            h_all[...] = h_hi[0] + h_hi[1]
+        else:
+            h_all[...] = h_gate[...]
+        for j in range(1, nz):
+            all_share(lax.rem(gate + j, nz)).start()
+
     for r in range(tiles):
         at = slice(r * tile, (r + 1) * tile)
         qt_s[:, at] = q_s[at].astype(jnp.float32).T.astype(jnp.bfloat16)
@@ -379,26 +501,19 @@
 
             line_sum(at, zb, 1).start()
 
-    hs_ref[...] = jnp.zeros_like(hs_ref)
-    hx[x] = jnp.zeros((group, tok), jnp.float32)
 
     def backward_chunk(i):
         key_rows = chunk_rows(row(i), 0)
-        hs_total = hx[x]
         for r in range(tiles):
             at = slice(r * tile, (r + 1) * tile)
             norm, delta = m_s[at], l_s[at]
             for b in range(NX):
                 cols = slice(b * tok, (b + 1) * tok)
-                centred = s_s[i, at, cols] - norm
-                prob = jnp.exp(centred)
+                prob = jnp.exp(s_s[i, at, cols] - norm)
                 d_score = prob * (dp_s[i, at, cols] - delta)
                 p_s[at, cols] = prob.astype(jnp.bfloat16)
                 ds_s[at, cols] = d_score.astype(jnp.bfloat16)
-                terms = (d_score * centred).reshape(tile // group, group, tok)
-                hs_total = hs_total + jnp.sum(terms, axis=0)
             acc_s[at] = acc_s[at] + nn_dot(ds_s[at], key_rows)
-        hx[x] = hs_total
         d_key = nn_dot(qt_s[...], ds_s[...])
         d_value = nn_dot(dot_s[...], p_s[...])
         for b in range(NX):
@@ -406,21 +521,6 @@
             part[i, b, 0] = d_key[:, cols].astype(jnp.bfloat16)
             part[i, b, 1] = d_value[:, cols].astype(jnp.bfloat16)
 
-    def hx_copy(s):
-        return remote(
-            hx.at[x], hx.at[x], hx_send.at[s], hx_recv.at[x], x_dev(s)
-        )
-
-    def hz_copy(j):
-        return remote(hz.at[z], hz.at[z], hz_send.at[j], hz_recv.at[z], z_dev(j))
-
-    def far_copy(t):
-        slot = ki * nd + di
-        return remote(hd_s.at[slot], hd_s.at[slot], hd_send.at[t], hd_recv.at[slot], far_dev(t))
-
-    def arrived(buffer, sems, slot):
-        remote(buffer.at[slot], buffer.at[slot], sems.at[slot], sems.at[slot], x_dev(1)).wait_recv()
-
     def scatter_step(k, carry):
         @pl.when(k < nz)
         def _():
@@ -433,8 +533,6 @@
 
         @pl.when(k == nz - 1)
         def _():
-            for s in range(1, NX):
-                hx_copy(s).start()
             for r in range(tiles):
                 at = slice(r * tile, (r + 1) * tile)
                 dq_s[at] = acc_s[at].astype(jnp.bfloat16)
@@ -457,24 +555,21 @@
                     along_line(nz // 2 - f)
                 to_mate(nz // 2 - 1 - f)
 
-        @pl.when(k == nz)
-        def _():
-            for s in range(1, NX):
-                arrived(hx, hx_recv, (x + s) % NX)
-            hz[z] = (hx[0] + hx[1]) + (hx[2] + hx[3])
-            for j in range(1, nz):
-                hz_copy(j).start()
-
-        @pl.when(k == nz + 2)
-        def _():
-            for j in range(1, nz):
-                arrived(hz, hz_recv, row(j))
-            hs_line = hz[0]
-            for j in range(1, nz):
-                hs_line = hs_line + hz[j]
-            hd_s[ki * nd + di] = hs_line
-            for t in range(1, nk * nd):
-                far_copy(t).start()
+        @pl.when(k == 1)
+        def _():
+            share_plane()
+
+        @pl.when(k == 4)
+        def _():
+            share_line()
+
+        @pl.when((k == nz) & at_gate)
+        def _():
+            share_across()
+
+        @pl.when((k == nz + 2) & at_gate)
+        def _():
+            share_all()
 
         return carry
 
@@ -499,20 +594,28 @@
     dk_ref[...] = part[0, x, 0].astype(jnp.float32).T.astype(jnp.bfloat16)
     dv_ref[...] = part[0, x, 1].astype(jnp.float32).T.astype(jnp.bfloat16)
 
-    for t in range(1, nk * nd):
-        arrived(hd_s, hd_recv, ((ki + t // nd) % nk) * nd + (di + t % nd) % nd)
+    @pl.when(jnp.logical_not(at_gate))
+    def _():
+        arrived(h_all, ha_recv.at[0])
+
     for kk in range(nk):
-        head_total = hd_s[kk * nd]
-        for dd in range(1, nd):
-            head_total = head_total + hd_s[kk * nd + dd]
-        hs_ref[kk * group : (kk + 1) * group] = head_total
-
-    for s in range(1, NX):
-        hx_copy(s).wait_send()
-    for j in range(1, nz):
-        hz_copy(j).wait_send()
-    for t in range(1, nk * nd):
-        far_copy(t).wait_send()
+        hs_ref[kk * group : (kk + 1) * group] = h_all[kk]
+
+    for t in range(1, nk):
+        kv_share(t).wait_send()
+    for t in range(1, NX * cores):
+        plane_share(t).wait_send()
+
+    @pl.when(at_gate)
+    def _():
+        if nd > cores:
+            across_share().wait_send()
+        for j in range(1, nz):
+            all_share(lax.rem(gate + j, nz)).wait_send()
+
+    @pl.when(jnp.logical_not(at_gate))
+    def _():
+        line_share().wait_send()
 
     def drain(j, carry):
         for side in range(2):
@@ -552,6 +655,24 @@
     lax.fori_loop(0, nz, drain, 0)
     out_copy.wait()
     dq_copy.wait()
+
+
+def results(out_in, dq_in, dk_in, dv_in, hs_in, scale_in, out, dq, dk, dv, d_scale, buffers, sem):
+    pairs = ((out_in, out), (dq_in, dq), (dk_in, dk), (dv_in, dv))
+    rows = [pair[0].shape[0] for pair in pairs]
+    views = [buffers.at[pl.ds(sum(rows[:i]), rows[i])] for i in range(4)]
+    loads = [pltpu.make_async_copy(pairs[i][0], views[i], sem.at[0, i]) for i in range(4)]
+    stores = [pltpu.make_async_copy(views[i], pairs[i][1], sem.at[1, i]) for i in range(4)]
+    for load in loads:
+        load.start()
+    totals = jnp.sum(hs_in[...].T, axis=0, keepdims=True)
+    scales = scale_in[...]
+    d_scale[...] = totals * math.sqrt(out_in.shape[1]) / (scales * scales)
+    for load, store in zip(loads, stores):
+        load.wait()
+        store.start()
+    for store in stores:
+        store.wait()
 
 
 def local(queries, keys, values, d_out, head_scale, doc_lengths, span_order):
@@ -588,6 +709,9 @@
             pltpu.VMEM((rows, hd), f32),
             pltpu.VMEM((rows, hd), f32),
             pltpu.VMEM((rows, hd), f32),
+            pltpu.VMEM((rows, hd), f32),
+            pltpu.VMEM((rows, hd), f32),
+            pltpu.VMEM((rows, hd), f32),
             pltpu.VMEM((rows, hd), bf),
             pltpu.VMEM((rows, hd), bf),
             pltpu.VMEM((rows, chunk), bf),
@@ -596,9 +720,14 @@
             pltpu.VMEM((nz, 2, hd, tok), bf),
             pltpu.VMEM((nz, 2, 2, hd, tok), bf),
             pltpu.VMEM((3, nz, 2, hd, tok), bf),
-            pltpu.VMEM((NX, group, tok), f32),
-            pltpu.VMEM((nz, group, tok), f32),
-            pltpu.VMEM((nk * nd, group, tok), f32),
+            pltpu.VMEM((group, hd), f32),
+            pltpu.VMEM((nk, group, hd), f32),
+            pltpu.VMEM((2 * NX, nk, group, hd), f32),
+            pltpu.VMEM((nk, group, hd), f32),
+            pltpu.VMEM((nz, nk, group, hd), f32),
+            pltpu.VMEM((nk, group, hd), f32),
+            pltpu.VMEM((2, nk, group, hd), f32),
+            pltpu.VMEM((nk, group, hd), f32),
             dma((4,)),
             dma((nz, NX, 2)),
             dma((3, nz)),
@@ -610,12 +739,12 @@
             dma((nz, 2, 2)),
             dma((3, nz)),
             dma((3, nz)),
-            dma((NX,)),
-            dma((NX,)),
+            dma((5, 2 * NX)),
+            dma((nk,)),
+            dma((2 * NX,)),
             dma((nz,)),
-            dma((nz,)),
-            dma((nk * nd,)),
-            dma((nk * nd,)),
+            dma((2,)),
+            dma((1,)),
         ],
         compiler_params=pltpu.CompilerParams(
             collective_id=0, has_side_effects=True, vmem_limit_bytes=60 * 1024 * 1024
@@ -629,13 +758,25 @@
         doc_lengths,
         span_order,
     )
-    d_head_scale = jnp.sum(hs, axis=1) * math.sqrt(hd) / (head_scale * head_scale)
+    out, dq, dk, dv, d_head_scale = pl.pallas_call(
+        results,
+        out_shape=(
+            jax.ShapeDtypeStruct((rows, hd), bf),
+            jax.ShapeDtypeStruct((rows, hd), bf),
+            jax.ShapeDtypeStruct((tok, hd), bf),
+            jax.ShapeDtypeStruct((tok, hd), bf),
+            jax.ShapeDtypeStruct((1, nk * group), f32),
+        ),
+        in_specs=[any_spec] * 4 + [vmem_spec] * 2,
+        out_specs=(any_spec, any_spec, any_spec, any_spec, vmem_spec),
+        scratch_shapes=[pltpu.VMEM((2 * (rows + tok), hd), bf), dma((2, 4))],
+    )(out, dq, dk, dv, hs, head_scale.reshape(1, nk * group))
     return (
         out.reshape(queries.shape),
         dq.reshape(queries.shape),
         dk.reshape(keys.shape),
         dv.reshape(values.shape),
-        d_head_scale,
+        d_head_scale.reshape(head_scale.shape),
     )
 
 

time: 95 us -> 82.1 us (0.86)
  the two profiles are of different devices: /device:TPU:1 before, /device:TPU:64 now
where the time goes in v3:
time: 82.1 us; the launch traced here: 81.9 us
  Pallas kernels  81.3 us (99%)
    pallas_call x1, Pallas kernels, local(): pl.pallas_call(functools.partial(kernel, group, tok, hd, doc_lengths.shap...  78.2 us
    pallas_call x1, Pallas kernels, local(): pl.pallas_call(results, out_shape=(jax.ShapeDtypeStruct((rows, hd), bf),...  3.05 us

profile of v3, /device:TPU:64, one launch (start us, length us, event | category | flops | bytes accessed | tf_op | source)
XLA Modules:
  0.0 81.9 jit_solution(5703547501763745931)
XLA Ops:
  0.6 78.2 %shard_map.110 = (bf16[1024,128]{1,0:T(8,128)(2,1)}, bf16[1024,128]{1,0:T(8,128)(2,1)}, bf16[128,128]{1,0:T(8,128)(2,1)}, bf16[128,128]{1,0:T(8,128)(2,1)}, f32[32,128]{1,0:T(8,128)}) custom-call(bf16[1024,128]{1,0:T(8,128)(2,1)} %bitcast.10, bf16[128,128]{1,0:T(8,128)(2,1)} %bitcast.12, bf16[128,128]{1,0:T(8,128)(2,1)} %bitcast.13, ...), custom_call_target="tpu_custom_call" | custom-call | tf_op jit(solution)/shard_map/pallas_call | solution.py:688
  78.9 3.0 %shard_map.111 = (bf16[1024,128]{1,0:T(8,128)(2,1)}, bf16[1024,128]{1,0:T(8,128)(2,1)}, bf16[128,128]{1,0:T(8,128)(2,1)}, bf16[128,128]{1,0:T(8,128)(2,1)}, f32[1,32]{1,0:T(1,128)}) custom-call(bf16[1024,128]{1,0:T(8,128)(2,1)} %get-tuple-element.15.out_in, bf16[1024,128]{1,0:T(8,128)(2,1)} %get-tuple-element.16.dq_in, ...), custom_call_target="tpu_custom_call" | custom-call | tf_op jit(solution)/shard_map/pallas_call | solution.py:761

commit v4 on v3

--- a/solution.py
+++ b/solution.py
@@ -10,8 +10,11 @@
 
 MESH = pl.DeviceIdType.MESH
 masked_low = -1e30
+hidden = -16384.0
 NX = 4
 X_LAG = 2
+RELAY_LAG = 2
+ROW_LAG = 4
 
 
 def nt_dot(a, b):
@@ -34,7 +37,7 @@
     group, tok, hd, docs, nk, nd,
     q_hbm, k_hbm, v_hbm, do_hbm, scale_ref, docs_ref, span_ref,
     out_hbm, dq_hbm, dk_ref, dv_ref, hs_ref,
-    q_s, do_s, qt_s, dot_s, kv, s_s, dp_s, row_lo, row_hi, m_s, l_s, wu_s, wd_s, wdu_s, acc_s,
+    q_s, qf_s, do_s, qt_s, dot_s, kv, s_s, dp_s, row_lo, row_hi, m_s, l_s, wu_s, wd_s, wdu_s, acc_s,
     out_s, dq_s, p_s, ds_s, part, rxa, rxc, rz, h_own, h_kv, h_plane, h_own_all, h_line, h_gate, h_hi, h_all,
     in_sem, g_recv, gz_send, gx_send, gr_send, a_send, a_recv,
     c_send, c_recv, z_send, z_recv,
@@ -126,17 +129,20 @@
             device_id_type=MESH,
         )
 
-    def block_copy(at, send_sem, device):
-        return remote(kv.at[at], kv.at[at], send_sem, g_recv.at[at[0], at[1], 0], device)
-
-    def line_copy(origin, side):
-        return block_copy((origin, x), gz_send.at[side, origin], up if side == 0 else down)
-
-    def mate_copy(origin):
-        return block_copy((origin, x), gz_send.at[2, origin], mate)
-
-    def x_copy(zb, bx, side):
-        return block_copy((zb, bx), gx_send.at[side, zb], right if side == 0 else left)
+    def piece_copy(zb, bx, piece, send_sem, device):
+        at = (zb, bx, piece)
+        return remote(kv.at[at], kv.at[at], send_sem, g_recv.at[at], device)
+
+    def line_copy(origin, side, piece):
+        sem = gz_send.at[side, origin, piece]
+        return piece_copy(origin, x, piece, sem, up if side == 0 else down)
+
+    def mate_copy(origin, piece):
+        return piece_copy(origin, x, piece, gz_send.at[2, origin, piece], mate)
+
+    def x_copy(zb, bx, side, piece):
+        sem = gx_send.at[side, zb, piece]
+        return piece_copy(zb, bx, piece, sem, right if side == 0 else left)
 
     def relay_copy(zb, bx, side):
         at = (zb, bx, side)
@@ -145,56 +151,63 @@
         )
 
     def x_sends(zb):
-        x_copy(zb, x, 0).start()
-        x_copy(zb, x, 1).start()
+        for side, piece in ((0, 0), (1, 1), (0, 1), (1, 0)):
+            x_copy(zb, x, side, piece).start()
 
     def relays(zb):
-        x_copy(zb, xl, 0).wait_recv()
+        x_copy(zb, xl, 0, 0).wait_recv()
         relay_copy(zb, xl, 0).start()
-        x_copy(zb, xr, 1).wait_recv()
+        x_copy(zb, xr, 1, 1).wait_recv()
         relay_copy(zb, xr, 1).start()
 
     def row_waits(zb):
+        x_copy(zb, xl, 0, 1).wait_recv()
+        x_copy(zb, xr, 1, 0).wait_recv()
         relay_copy(zb, xo, 0).wait_recv()
         relay_copy(zb, xo, 1).wait_recv()
 
-    def forward_line(origin, side):
+    def forward_line(origin, side, piece):
         @pl.when((z < nz - 2) if side == 0 else (z >= 2))
         def _():
-            line_copy(origin, side).start()
+            line_copy(origin, side, piece).start()
 
     def line_step(e):
         if e < nz // 2:
-
-            @pl.when(z >= 2 * e)
-            def _():
-                line_copy(z - 2 * e, 0).wait_recv()
-                forward_line(z - 2 * e, 0)
-                mate_copy(z - 2 * e).start()
-
-            @pl.when(z + 2 * e < nz)
-            def _():
-                line_copy(z + 2 * e, 1).wait_recv()
-                forward_line(z + 2 * e, 1)
-                mate_copy(z + 2 * e).start()
-
-        if e == 1:
-            mate_copy(zp).wait_recv()
-        else:
-
-            @pl.when(zp >= 2 * (e - 1))
-            def _():
-                mate_copy(zp - 2 * (e - 1)).wait_recv()
-
-            @pl.when(zp + 2 * (e - 1) < nz)
-            def _():
-                mate_copy(zp + 2 * (e - 1)).wait_recv()
+            for piece in range(2):
+
+                @pl.when(z >= 2 * e)
+                def _():
+                    line_copy(z - 2 * e, 0, piece).wait_recv()
+                    forward_line(z - 2 * e, 0, piece)
+                    mate_copy(z - 2 * e, piece).start()
+
+                @pl.when(z + 2 * e < nz)
+                def _():
+                    line_copy(z + 2 * e, 1, piece).wait_recv()
+                    forward_line(z + 2 * e, 1, piece)
+                    mate_copy(z + 2 * e, piece).start()
+
+        for piece in range(2):
+            if e == 1:
+                mate_copy(zp, piece).wait_recv()
+            else:
+
+                @pl.when(zp >= 2 * (e - 1))
+                def _():
+                    mate_copy(zp - 2 * (e - 1), piece).wait_recv()
+
+                @pl.when(zp + 2 * (e - 1) < nz)
+                def _():
+                    mate_copy(zp + 2 * (e - 1), piece).wait_recv()
 
     k_in.wait()
+    forward_line(z, 0, 0)
+    forward_line(z, 1, 0)
     v_in.wait()
-    forward_line(z, 0)
-    forward_line(z, 1)
-    mate_copy(z).start()
+    forward_line(z, 0, 1)
+    forward_line(z, 1, 1)
+    mate_copy(z, 0).start()
+    mate_copy(z, 1).start()
     x_sends(z)
 
     head0 = ki * group
@@ -213,6 +226,15 @@
         running = running + docs_ref[0, d]
         bounds.append(running)
     first_span, second_span = span_ref[2 * me], span_ref[2 * me + 1]
+
+    blocks = span_ref.shape[0]
+    lane1 = lax.broadcasted_iota(jnp.int32, (1, hd), 1)
+    doc_low = jnp.full((1, hd), 1 << 30, jnp.int32)
+    doc_high = jnp.zeros((1, hd), jnp.int32)
+    for d in range(docs):
+        doc_low = jnp.where(lane1 == blocks + d, bounds[d - 1] if d else 0, doc_low)
+        doc_high = jnp.where(lane1 == blocks + d, bounds[d], doc_high)
+    doc_lane = (lane1 >= blocks) & (lane1 < blocks + docs)
 
     def row_values(r, carry):
         base = r * tile
@@ -223,6 +245,10 @@
             low = jnp.maximum(low, jnp.where(place >= bound, bound, 0))
         at = pl.ds(pl.multiple_of(base, tile), tile)
         row_hi[at] = place
+        lane = lax.broadcasted_iota(jnp.int32, (tile, hd), 1)
+        later = (lane < blocks) & (lane * span > place)
+        other = doc_lane & ((place < doc_low) | (place >= doc_high))
+        qf_s[at] = jnp.where(later | other, hidden, 0.0).astype(jnp.bfloat16)
         row_lo[at] = low
         m_s[at] = jnp.full((tile, hd), masked_low, jnp.float32)
         for total in (l_s, wu_s, wd_s, wdu_s, acc_s):
@@ -236,27 +262,35 @@
     def chunk_rows(zb, which):
         return kv[zb, :, which].reshape(chunk, hd)
 
-    def forward_chunk(i, zb):
+    def forward_chunk(i, zb, own):
         key_rows, value_rows = chunk_rows(zb, 0), chunk_rows(zb, 1)
         lane = lax.broadcasted_iota(jnp.int32, (group, tok), 1)
-        places = []
+        key_lane = lax.broadcasted_iota(jnp.int32, (tok, hd), 1)
+        key_row = lax.broadcasted_iota(jnp.int32, (tok, hd), 0)
+        places, features = [], []
         for b in range(NX):
             owner = zb * NX + b
-            lower = span_ref[owner * 2] * span
-            upper = span_ref[owner * 2 + 1] * span - span
-            place = jnp.where(lane < span, lower, upper) + lane
+            lower, upper = span_ref[owner * 2], span_ref[owner * 2 + 1]
+            block = jnp.where(key_row < span, lower, upper)
+            key_place = block * span + jnp.where(key_row < span, key_row, key_row - span)
+            marked = (key_lane == block) | ((key_place >= doc_low) & (key_place < doc_high))
+            features.append(jnp.where(marked, 1.0, 0.0).astype(jnp.bfloat16))
+            place = jnp.where(lane < span, lower * span, upper * span - span) + lane
             places.append(
                 jnp.broadcast_to(place[None], (tile // group, group, tok)).reshape(tile, tok)
             )
+        key_rows = jnp.concatenate([key_rows, jnp.concatenate(features, axis=0)], axis=1)
         factor = per_row(factor8)
         for r in range(tiles):
             at = slice(r * tile, (r + 1) * tile)
-            raw = nt_dot(q_s[at], key_rows)
+            raw = nt_dot(jnp.concatenate([q_s[at], qf_s[at]], axis=1), key_rows)
             low, high = row_lo[at], row_hi[at]
             scores = []
             for b in range(NX):
-                visible = (places[b] >= low) & (places[b] <= high)
-                score = jnp.where(visible, raw[:, b * tok : (b + 1) * tok] * factor, masked_low)
+                score = raw[:, b * tok : (b + 1) * tok] * factor
+                if own:
+                    visible = (places[b] >= low) & (places[b] <= high)
+                    score = jnp.where(visible, score, masked_low)
                 s_s[i, at, b * tok : (b + 1) * tok] = score
                 scores.append(score)
             peak = jnp.maximum(
@@ -273,10 +307,10 @@
                 cols = slice(b * tok, (b + 1) * tok)
                 below = scores[b] - new
                 weight = jnp.exp(below)
-                d_scaled = d_prob[:, cols] * factor
+                d_here = d_prob[:, cols]
                 p_s[at, cols] = weight.astype(jnp.bfloat16)
-                dp_s[i, at, cols] = d_scaled
-                weighted = weight * d_scaled
+                dp_s[i, at, cols] = d_here
+                weighted = weight * d_here
                 w_sum, wu_sum = w_sum + weight, wu_sum + weight * below
                 wd_sum, wdu_sum = wd_sum + weighted, wdu_sum + weighted * below
             w_old, wd_old = l_s[at], wd_s[at]
@@ -288,6 +322,13 @@
         acc_s[...] = acc_s[...] + nn_dot(p_s[...], value_rows)
 
     def gather_step(i, carry):
+        @pl.when(i == 0)
+        def _():
+            for r in range(tiles):
+                at = slice(r * tile, (r + 1) * tile)
+                qt_s[:, at] = q_s[at].astype(jnp.float32).T.astype(jnp.bfloat16)
+                dot_s[:, at] = do_s[at].astype(jnp.float32).T.astype(jnp.bfloat16)
+
         for e in range(1, nz // 2 + 1):
 
             @pl.when(i == 2 * e - 1)
@@ -298,19 +339,26 @@
         def _():
             x_sends(row(i))
 
-        @pl.when((i >= X_LAG) & (i < nz + X_LAG))
-        def _():
-            relays(row(i - X_LAG))
-
-        @pl.when(i >= 2 * X_LAG)
-        def _():
-            zb = row(i - 2 * X_LAG)
+        @pl.when((i >= RELAY_LAG) & (i < nz + RELAY_LAG))
+        def _():
+            relays(row(i - RELAY_LAG))
+
+        @pl.when(i >= ROW_LAG)
+        def _():
+            zb = row(i - ROW_LAG)
             row_waits(zb)
-            forward_chunk(i - 2 * X_LAG, zb)
+
+            @pl.when(i == ROW_LAG)
+            def _():
+                forward_chunk(0, zb, True)
+
+            @pl.when(i > ROW_LAG)
+            def _():
+                forward_chunk(i - ROW_LAG, zb, False)
 
         return carry
 
-    lax.fori_loop(0, nz + 2 * X_LAG, gather_step, 0)
+    lax.fori_loop(0, nz + ROW_LAG, gather_step, 0)
 
     def finish_rows(r, hs_total):
         at = pl.ds(pl.multiple_of(r * tile, tile), tile)
@@ -321,9 +369,9 @@
         out_s[at] = out_rows
         m_s[at] = m_s[at] + log_total
         product = do_s[at].astype(jnp.float32) * out_rows.astype(jnp.float32)
-        delta = jnp.sum(product, axis=1, keepdims=True) * per_row(factor8)
+        delta = jnp.sum(product, axis=1, keepdims=True)
         terms = wdu_s[at] - delta * wu_s[at] - log_total * (wd_s[at] - delta * weights)
-        l_s[at] = delta
+        l_s[at] = jnp.broadcast_to(delta, (tile, hd))
         acc_s[at] = jnp.zeros((tile, hd), jnp.float32)
         return hs_total + jnp.sum((terms / total).reshape(tile // group, group, hd), axis=0)
 
@@ -405,10 +453,6 @@
         for j in range(1, nz):
             all_share(lax.rem(gate + j, nz)).start()
 
-    for r in range(tiles):
-        at = slice(r * tile, (r + 1) * tile)
-        qt_s[:, at] = q_s[at].astype(jnp.float32).T.astype(jnp.bfloat16)
-        dot_s[:, at] = do_s[at].astype(jnp.float32).T.astype(jnp.bfloat16)
 
     def a_copy(j, side):
         return remote(
@@ -428,14 +472,23 @@
             left if side == 0 else right,
         )
 
-    def line_sum(j, zb, side):
+    def line_sum(j, zb, side, piece):
         return remote(
-            part.at[j, x], rz.at[side, zb], z_send.at[side, zb], z_recv.at[side, zb],
+            part.at[j, x, piece],
+            rz.at[side, zb, piece],
+            z_send.at[side, zb, piece],
+            z_recv.at[side, zb, piece],
             up if side == 0 else down,
         )
 
-    def mate_sum(j, zb):
-        return remote(part.at[j, x], rz.at[2, zb], z_send.at[2, zb], z_recv.at[2, zb], mate)
+    def mate_sum(j, zb, piece):
+        return remote(
+            part.at[j, x, piece],
+            rz.at[2, zb, piece],
+            z_send.at[2, zb, piece],
+            z_recv.at[2, zb, piece],
+            mate,
+        )
 
     def add_bf(a, b):
         return (a.astype(jnp.float32) + b.astype(jnp.float32)).astype(jnp.bfloat16)
@@ -458,7 +511,9 @@
 
     def to_mate(s):
         def send(target):
-            mate_sum(2 * xor_index(pair, target, nz // 2) + 1, zp + 2 * (target - pair)).start()
+            for piece in range(2):
+                at = 2 * xor_index(pair, target, nz // 2) + 1
+                mate_sum(at, zp + 2 * (target - pair), piece).start()
 
         if s == 0:
             send(pair)
@@ -473,44 +528,33 @@
                 send(pair - s)
 
     def along_line(s):
-        @pl.when(pair + s < nz // 2)
-        def _():
-            zb = z + 2 * s
-            at = 2 * xor_index(pair, pair + s, nz // 2)
-            mate_sum(at, zb).wait_recv()
-            part[at, x] = add_bf(part[at, x], rz[2, zb])
-
-            @pl.when(pair > 0)
-            def _():
-                line_sum(at, zb, 0).wait_recv()
-                part[at, x] = add_bf(part[at, x], rz[0, zb])
-
-            line_sum(at, zb, 0).start()
-
-        @pl.when(pair >= s)
-        def _():
-            zb = z - 2 * s
-            at = 2 * xor_index(pair, pair - s, nz // 2)
-            mate_sum(at, zb).wait_recv()
-            part[at, x] = add_bf(part[at, x], rz[2, zb])
-
-            @pl.when(pair < nz // 2 - 1)
-            def _():
-                line_sum(at, zb, 1).wait_recv()
-                part[at, x] = add_bf(part[at, x], rz[1, zb])
-
-            line_sum(at, zb, 1).start()
-
+        for piece in range(2):
+            for side, far in ((0, s), (1, -s)):
+
+                @pl.when((pair + s < nz // 2) if side == 0 else (pair >= s))
+                def _():
+                    zb = z + 2 * far
+                    at = 2 * xor_index(pair, pair + far, nz // 2)
+                    mate_sum(at, zb, piece).wait_recv()
+                    part[at, x, piece] = add_bf(part[at, x, piece], rz[2, zb, piece])
+
+                    @pl.when((pair > 0) if side == 0 else (pair < nz // 2 - 1))
+                    def _():
+                        line_sum(at, zb, side, piece).wait_recv()
+                        part[at, x, piece] = add_bf(part[at, x, piece], rz[side, zb, piece])
+
+                    line_sum(at, zb, side, piece).start()
 
     def backward_chunk(i):
         key_rows = chunk_rows(row(i), 0)
+        factor = per_row(factor8)
         for r in range(tiles):
             at = slice(r * tile, (r + 1) * tile)
             norm, delta = m_s[at], l_s[at]
             for b in range(NX):
                 cols = slice(b * tok, (b + 1) * tok)
                 prob = jnp.exp(s_s[i, at, cols] - norm)
-                d_score = prob * (dp_s[i, at, cols] - delta)
+                d_score = prob * ((dp_s[i, at, cols] - delta) * factor)
                 p_s[at, cols] = prob.astype(jnp.bfloat16)
                 ds_s[at, cols] = d_score.astype(jnp.bfloat16)
             acc_s[at] = acc_s[at] + nn_dot(ds_s[at], key_rows)
@@ -576,19 +620,20 @@
     dq_copy = pltpu.make_async_copy(dq_s, dq_hbm, in_sem.at[1])
     lax.fori_loop(0, nz + 2 * X_LAG, scatter_step, 0)
 
-    total = part[0, x].astype(jnp.float32)
-    mate_sum(0, z).wait_recv()
-    rz_own = rz[2, z].astype(jnp.float32)
-    part[0, x] = (total + rz_own).astype(jnp.bfloat16)
+    for piece in range(2):
+        mate_sum(0, z, piece).wait_recv()
+    part[0, x] = add_bf(part[0, x], rz[2, z])
 
     @pl.when(pair > 0)
     def _():
-        line_sum(0, z, 0).wait_recv()
+        for piece in range(2):
+            line_sum(0, z, 0, piece).wait_recv()
         part[0, x] = add_bf(part[0, x], rz[0, z])
 
     @pl.when(pair < nz // 2 - 1)
     def _():
-        line_sum(0, z, 1).wait_recv()
+        for piece in range(2):
+            line_sum(0, z, 1, piece).wait_recv()
         part[0, x] = add_bf(part[0, x], rz[1, z])
 
     dk_ref[...] = part[0, x, 0].astype(jnp.float32).T.astype(jnp.bfloat16)
@@ -619,36 +664,37 @@
 
     def drain(j, carry):
         for side in range(2):
-            x_copy(j, x, side).wait_send()
             relay_copy(j, xl, side).wait_send()
             a_copy(j, side).wait_send()
             for piece in range(2):
+                x_copy(j, x, side, piece).wait_send()
                 c_copy(j, side, piece).wait_send()
         same = lax.rem(z + j, 2) == 0
-
-        @pl.when(same)
-        def _():
-            mate_copy(j).wait_send()
-
-            @pl.when((j <= z) & (z < nz - 2))
+        for piece in range(2):
+
+            @pl.when(same)
             def _():
-                line_copy(j, 0).wait_send()
-
-            @pl.when((j >= z) & (z >= 2))
+                mate_copy(j, piece).wait_send()
+
+                @pl.when((j <= z) & (z < nz - 2))
+                def _():
+                    line_copy(j, 0, piece).wait_send()
+
+                @pl.when((j >= z) & (z >= 2))
+                def _():
+                    line_copy(j, 1, piece).wait_send()
+
+                @pl.when(j > z)
+                def _():
+                    line_sum(0, j, 0, piece).wait_send()
+
+                @pl.when(j < z)
+                def _():
+                    line_sum(0, j, 1, piece).wait_send()
+
+            @pl.when(jnp.logical_not(same))
             def _():
-                line_copy(j, 1).wait_send()
-
-            @pl.when(j > z)
-            def _():
-                line_sum(0, j, 0).wait_send()
-
-            @pl.when(j < z)
-            def _():
-                line_sum(0, j, 1).wait_send()
-
-        @pl.when(jnp.logical_not(same))
-        def _():
-            mate_sum(0, j).wait_send()
+                mate_sum(0, j, piece).wait_send()
 
         return carry
 
@@ -667,7 +713,7 @@
         load.start()
     totals = jnp.sum(hs_in[...].T, axis=0, keepdims=True)
     scales = scale_in[...]
-    d_scale[...] = totals * math.sqrt(out_in.shape[1]) / (scales * scales)
+    d_scale[...] = totals / scales
     for load, store in zip(loads, stores):
         load.wait()
         store.start()
@@ -697,6 +743,7 @@
         in_specs=[any_spec] * 4 + [smem_spec] * 3,
         out_specs=(any_spec, any_spec, vmem_spec, vmem_spec, vmem_spec),
         scratch_shapes=[
+            pltpu.VMEM((rows, hd), bf),
             pltpu.VMEM((rows, hd), bf),
             pltpu.VMEM((rows, hd), bf),
             pltpu.VMEM((hd, rows), bf),
@@ -730,15 +777,15 @@
             pltpu.VMEM((nk, group, hd), f32),
             dma((4,)),
             dma((nz, NX, 2)),
-            dma((3, nz)),
-            dma((2, nz)),
+            dma((3, nz, 2)),
+            dma((2, nz, 2)),
             dma((2, nz)),
             dma((nz, 2)),
             dma((nz, 2)),
             dma((nz, 2, 2)),
             dma((nz, 2, 2)),
-            dma((3, nz)),
-            dma((3, nz)),
+            dma((3, nz, 2)),
+            dma((3, nz, 2)),
             dma((5, 2 * NX)),
             dma((nk,)),
             dma((2 * NX,)),

time: 82.1 us -> 80.4 us (0.979)
  Pallas kernels: 81.3 us -> 79.5 us
    pallas_call x1, Pallas kernels: 78.2 us -> 76.5 us  [local(): pl.pallas_call(functools.partial(kernel, group, tok, hd, doc_lengths.shap...]
where the time goes in v4:
time: 80.4 us; the launch traced here: 80.2 us
  Pallas kernels  79.5 us (99%)
    pallas_call x1, Pallas kernels, local(): pl.pallas_call(functools.partial(kernel, group, tok, hd, doc_lengths.shap...  76.5 us
    pallas_call x1, Pallas kernels, local(): pl.pallas_call(results, out_shape=(jax.ShapeDtypeStruct((rows, hd), bf),...  3.05 us

profile of v4, /device:TPU:64, one launch (start us, length us, event | category | flops | bytes accessed | tf_op | source)
XLA Modules:
  0.0 80.2 jit_solution(12969109921599461966)
XLA Ops:
  0.6 76.5 %shard_map.110 = (bf16[1024,128]{1,0:T(8,128)(2,1)}, bf16[1024,128]{1,0:T(8,128)(2,1)}, bf16[128,128]{1,0:T(8,128)(2,1)}, bf16[128,128]{1,0:T(8,128)(2,1)}, f32[32,128]{1,0:T(8,128)}) custom-call(bf16[1024,128]{1,0:T(8,128)(2,1)} %bitcast.10, bf16[128,128]{1,0:T(8,128)(2,1)} %bitcast.12, bf16[128,128]{1,0:T(8,128)(2,1)} %bitcast.13, ...), custom_call_target="tpu_custom_call" | custom-call | tf_op jit(solution)/shard_map/pallas_call | solution.py:734
  77.1 3.0 %shard_map.111 = (bf16[1024,128]{1,0:T(8,128)(2,1)}, bf16[1024,128]{1,0:T(8,128)(2,1)}, bf16[128,128]{1,0:T(8,128)(2,1)}, bf16[128,128]{1,0:T(8,128)(2,1)}, f32[1,32]{1,0:T(1,128)}) custom-call(bf16[1024,128]{1,0:T(8,128)(2,1)} %get-tuple-element.15.out_in, bf16[1024,128]{1,0:T(8,128)(2,1)} %get-tuple-element.16.dq_in, ...), custom_call_target="tpu_custom_call" | custom-call | tf_op jit(solution)/shard_map/pallas_call | solution.py:808

commit v5 on v4

--- a/solution.py
+++ b/solution.py
@@ -172,6 +172,20 @@
             line_copy(origin, side, piece).start()
 
     def line_step(e):
+        for piece in range(2):
+            if e == 1:
+                mate_copy(zp, piece).wait_recv()
+            else:
+
+                @pl.when(zp >= 2 * (e - 1))
+                def _():
+                    mate_copy(zp - 2 * (e - 1), piece).wait_recv()
+
+                @pl.when(zp + 2 * (e - 1) < nz)
+                def _():
+                    mate_copy(zp + 2 * (e - 1), piece).wait_recv()
+
+        x_sends(row(2 * e - 1))
         if e < nz // 2:
             for piece in range(2):
 
@@ -187,18 +201,7 @@
                     forward_line(z + 2 * e, 1, piece)
                     mate_copy(z + 2 * e, piece).start()
 
-        for piece in range(2):
-            if e == 1:
-                mate_copy(zp, piece).wait_recv()
-            else:
-
-                @pl.when(zp >= 2 * (e - 1))
-                def _():
-                    mate_copy(zp - 2 * (e - 1), piece).wait_recv()
-
-                @pl.when(zp + 2 * (e - 1) < nz)
-                def _():
-                    mate_copy(zp + 2 * (e - 1), piece).wait_recv()
+            x_sends(row(2 * e))
 
     k_in.wait()
     forward_line(z, 0, 0)
@@ -334,10 +337,6 @@
             @pl.when(i == 2 * e - 1)
             def _():
                 line_step(e)
-
-        @pl.when((i > 0) & (i < nz))
-        def _():
-            x_sends(row(i))
 
         @pl.when((i >= RELAY_LAG) & (i < nz + RELAY_LAG))
         def _():

time: 80.4 us -> 82.7 us (1.029)
  Pallas kernels: 79.5 us -> 81.8 us
    pallas_call x1, Pallas kernels: 76.5 us -> 78.8 us  [local(): pl.pallas_call(functools.partial(kernel, group, tok, hd, doc_lengths.shap...]
where the time goes in v5:
time: 82.7 us; the launch traced here: 82.5 us
  Pallas kernels  81.8 us (99%)
    pallas_call x1, Pallas kernels, local(): pl.pallas_call(functools.partial(kernel, group, tok, hd, doc_lengths.shap...  78.8 us
    pallas_call x1, Pallas kernels, local(): pl.pallas_call(results, out_shape=(jax.ShapeDtypeStruct((rows, hd), bf),...  3.05 us

profile of v5, /device:TPU:64, one launch (start us, length us, event | category | flops | bytes accessed | tf_op | source)
XLA Modules:
  0.0 82.5 jit_solution(7104190811502113276)
XLA Ops:
  0.6 78.8 %shard_map.110 = (bf16[1024,128]{1,0:T(8,128)(2,1)}, bf16[1024,128]{1,0:T(8,128)(2,1)}, bf16[128,128]{1,0:T(8,128)(2,1)}, bf16[128,128]{1,0:T(8,128)(2,1)}, f32[32,128]{1,0:T(8,128)}) custom-call(bf16[1024,128]{1,0:T(8,128)(2,1)} %bitcast.10, bf16[128,128]{1,0:T(8,128)(2,1)} %bitcast.12, bf16[128,128]{1,0:T(8,128)(2,1)} %bitcast.13, ...), custom_call_target="tpu_custom_call" | custom-call | tf_op jit(solution)/shard_map/pallas_call | solution.py:733
  79.4 3.0 %shard_map.111 = (bf16[1024,128]{1,0:T(8,128)(2,1)}, bf16[1024,128]{1,0:T(8,128)(2,1)}, bf16[128,128]{1,0:T(8,128)(2,1)}, bf16[128,128]{1,0:T(8,128)(2,1)}, f32[1,32]{1,0:T(1,128)}) custom-call(bf16[1024,128]{1,0:T(8,128)(2,1)} %get-tuple-element.15.out_in, bf16[1024,128]{1,0:T(8,128)(2,1)} %get-tuple-element.16.dq_in, ...), custom_call_target="tpu_custom_call" | custom-call | tf_op jit(solution)/shard_map/pallas_call | solution.py:807
